TPU v7x, 32 devices: a whole 2x2x4 slice. The times are simulated.
32 devices in a mesh: dat: 4 (over z), seq: 8 (over y, x, core).
Axes of the slice: x: 2, y: 2, z: 4, core: 2. Of those that a mesh axis runs over, the one named last changes fastest.
Arguments:
- clip_latents: bfloat16 [8, 16, 256, 384], P('dat', 'seq'), may hold values from -6 to 6
- conditioning: bfloat16 [8, 384], P('dat'), may hold values from -6 to 6
- timesteps: int32 [8], P('dat'), may hold values from 0 to 999
- clip_live: int32 [8], P('dat'), may hold values 0 or 1
- cotangent: bfloat16 [8, 16, 256, 384], P('dat', 'seq'), may hold values from -6 to 6
- ada_weight: bfloat16 [2, 384, 2304], P(None, ('dat', 'seq')), may hold values from -0.3125 to 0.3125
- query_key_value_weight: bfloat16 [2, 384, 1152], P(None, ('dat', 'seq')), may hold values from -0.3125 to 0.3125
- output_projection_weight: bfloat16 [2, 384, 384], P(None, ('dat', 'seq')), may hold values from -1.25 to 1.25
- first_feedforward_weight: bfloat16 [2, 384, 1536], P(None, ('dat', 'seq')), may hold values from -0.3125 to 0.3125
- second_feedforward_weight: bfloat16 [2, 1536, 384], P(None, ('dat', 'seq')), may hold values from -0.15625 to 0.15625
- biases: bfloat16 [2, 5376], P(None, ('dat', 'seq')), may hold values from -3 to 3
Outputs:
- out_latents: float32 [8, 16, 256, 384], P('dat', 'seq')
- grad_latents: float32 [8, 16, 256, 384], P('dat', 'seq')
- grad_conditioning: float32 [8, 384], P('dat')
- grad_ada: float32 [2, 384, 2304], P(None, ('dat', 'seq'))
- grad_qkv: float32 [2, 384, 1152], P(None, ('dat', 'seq'))
- grad_proj: float32 [2, 384, 384], P(None, ('dat', 'seq'))
- grad_fc1: float32 [2, 384, 1536], P(None, ('dat', 'seq'))
- grad_fc2: float32 [2, 1536, 384], P(None, ('dat', 'seq'))
- grad_biases: float32 [2, 5376], P(None, ('dat', 'seq'))
All inputs are finite; a program needn't handle non-finite values. No bound on the sum of `clip_live` on one device may be relied on, other than what follows from the above.
Results may differ from a plain program's by a relative error of at most 0.025.
The roundings to bfloat16 on the way count: a program that leaves them out, or rounds other values in their place, can miss the bound.
Values may be sent and summed in bfloat16 or wider, within the bound.
No kernel may reach another device: no remote copies, remote signals or barrier semaphores. Data moves between devices by JAX's collectives and lax.ppermute only.
A program may use at most 128 MiB of HBM per device.

v0:
```python
from functools import partial
import math

import jax
import jax.numpy as jnp
from jax import lax
from jax.sharding import PartitionSpec as P

H = 6
HD = 64


ln_epsilon = 1e-06
highest = lax.Precision.HIGHEST


def layer_norm(values):
    center = values - jnp.mean(values, axis=-1, keepdims=True)
    spread = jnp.mean(center * center, axis=-1, keepdims=True)
    return center * lax.rsqrt(spread + ln_epsilon)


def modulated(values, shift, scaling):
    return layer_norm(values) * (1.0 + scaling) + shift


def timestep_embed(timestep, features):
    half_count = features // 2
    frequency = jnp.exp(-math.log(10000.0) * jnp.arange(half_count, dtype=jnp.float32) / half_count)
    angles = timestep.astype(jnp.float32) * frequency
    return jnp.concatenate([jnp.cos(angles), jnp.sin(angles)])


def score_forms(temporal_layer_flag):
    query_form = "sghd" if temporal_layer_flag else "gshd"
    key_form = "tghd" if temporal_layer_flag else "gthd"
    return (query_form, key_form)


def score_values(query, key_heads, temporal_layer_flag):
    query_form, key_form = score_forms(temporal_layer_flag)
    scaling = 1.0 / math.sqrt(query.shape[-1])
    scores = (
        jnp.einsum(
            query_form + "," + key_form + "->ghst",
            query,
            key_heads,
            preferred_element_type=jnp.float32,
        )
        * scaling
    )
    return (scores, scaling)


def attend(query, key_heads, value_heads, temporal_layer_flag):
    query_form, key_form = score_forms(temporal_layer_flag)
    scores, scaling = score_values(query, key_heads, temporal_layer_flag)
    peak_score = jnp.max(scores, axis=-1, keepdims=True)
    log_total = peak_score + jnp.log(jnp.sum(jnp.exp(scores - peak_score), axis=-1, keepdims=True))
    attn_probs = jnp.exp(scores - log_total).astype(jnp.bfloat16)
    attended = jnp.einsum(
        "ghst," + key_form + "->" + query_form,
        attn_probs,
        value_heads,
        preferred_element_type=jnp.float32,
    )
    return (attended, log_total)


def attend_back(query, key_heads, value_heads, log_total, grad_attended, temporal_layer_flag):
    query_form, key_form = score_forms(temporal_layer_flag)
    scores, scaling = score_values(query, key_heads, temporal_layer_flag)
    attn_probs = jnp.exp(scores - log_total)
    grad_values = jnp.einsum(
        "ghst," + query_form + "->" + key_form,
        attn_probs.astype(jnp.bfloat16),
        grad_attended,
        preferred_element_type=jnp.float32,
    )
    grad_probs = jnp.einsum(
        query_form + "," + key_form + "->ghst",
        grad_attended,
        value_heads,
        preferred_element_type=jnp.float32,
    )
    row_dots = jnp.sum(grad_probs * attn_probs, axis=-1, keepdims=True)
    grad_scores = (attn_probs * (grad_probs - row_dots)).astype(jnp.bfloat16)
    grad_query = (
        jnp.einsum(
            "ghst," + key_form + "->" + query_form,
            grad_scores,
            key_heads,
            preferred_element_type=jnp.float32,
        )
        * scaling
    )
    grad_keys = (
        jnp.einsum(
            "ghst," + query_form + "->" + key_form,
            grad_scores,
            query,
            preferred_element_type=jnp.float32,
        )
        * scaling
    )
    return (grad_query, grad_keys, grad_values)


def layer_forward(residual_stream, adaptive_modulation, params, temporal_layer_flag):
    (
        ada_weight,
        query_key_value_weight,
        output_projection_weight,
        first_feedforward_weight,
        second_feedforward_weight,
        bias_vector_row,
    ) = params
    features = residual_stream.shape[-1]
    outer_count, inner_count = (residual_stream.shape[0], residual_stream.shape[1])
    row_count = outer_count * inner_count
    hidden_count = first_feedforward_weight.shape[1]
    bias_float = bias_vector_row.astype(jnp.float32)
    shift_a, scale_a, gate_a, shift_b, scale_b, gate_b = jnp.split(adaptive_modulation, 6)
    token_rows = residual_stream.reshape(row_count, features)
    normed_a = modulated(token_rows, shift_a, scale_a).astype(jnp.bfloat16)
    query_bias = bias_float[6 * features : 7 * features]
    value_bias = bias_float[7 * features : 8 * features]
    qkv_bias = jnp.concatenate([query_bias, jnp.zeros_like(query_bias), value_bias])
    projected = (
        jnp.dot(normed_a, query_key_value_weight, preferred_element_type=jnp.float32) + qkv_bias
    ).astype(jnp.bfloat16)
    heads_all = projected.reshape(outer_count, inner_count, 3, H, HD)
    query, key_heads, value_heads = (heads_all[:, :, 0], heads_all[:, :, 1], heads_all[:, :, 2])
    attended, log_total = attend(query, key_heads, value_heads, temporal_layer_flag)
    attended = attended.reshape(row_count, features).astype(jnp.bfloat16)
    branch = (
        jnp.dot(attended, output_projection_weight, preferred_element_type=jnp.float32)
        + bias_float[8 * features : 9 * features]
    )
    midway = token_rows + gate_a * branch
    normed_b = modulated(midway, shift_b, scale_b).astype(jnp.bfloat16)
    hidden_pre = (
        jnp.dot(normed_b, first_feedforward_weight, preferred_element_type=jnp.float32)
        + bias_float[9 * features : 9 * features + hidden_count]
    )
    hidden_act = jax.nn.gelu(hidden_pre, approximate=True).astype(jnp.bfloat16)
    mlp_out = (
        jnp.dot(hidden_act, second_feedforward_weight, preferred_element_type=jnp.float32)
        + bias_float[9 * features + hidden_count :]
    )
    result = midway + gate_b * mlp_out
    kept = (
        token_rows,
        normed_a,
        query,
        key_heads,
        value_heads,
        log_total,
        attended,
        branch,
        midway,
        normed_b,
        hidden_pre,
        hidden_act,
        mlp_out,
    )
    return (result.reshape(outer_count, inner_count, features), kept)


def layer_backward(gradient, adaptive_modulation, params, kept, temporal_layer_flag):
    (
        ada_weight,
        query_key_value_weight,
        output_projection_weight,
        first_feedforward_weight,
        second_feedforward_weight,
        bias_vector_row,
    ) = params
    (
        token_rows,
        normed_a,
        query,
        key_heads,
        value_heads,
        log_total,
        attended,
        branch,
        midway,
        normed_b,
        hidden_pre,
        hidden_act,
        mlp_out,
    ) = kept
    shape_in = gradient.shape
    features = shape_in[-1]
    row_count = token_rows.shape[0]
    shift_a, scale_a, gate_a, shift_b, scale_b, gate_b = jnp.split(adaptive_modulation, 6)
    grad_rows = gradient.reshape(row_count, features)
    grad_mlp = (gate_b * grad_rows).astype(jnp.bfloat16)
    grad_gate_b = jnp.sum(grad_rows * mlp_out, axis=0)
    grad_fc2 = jnp.einsum("nf,nd->fd", hidden_act, grad_mlp, preferred_element_type=jnp.float32)
    grad_fc2_bias = jnp.sum(grad_mlp, axis=0, dtype=jnp.float32)
    grad_act = jnp.einsum(
        "nd,fd->nf", grad_mlp, second_feedforward_weight, preferred_element_type=jnp.float32
    )
    gelu_value, gelu_pull = jax.vjp(partial(jax.nn.gelu, approximate=True), hidden_pre)
    grad_pre = gelu_pull(grad_act)[0].astype(jnp.bfloat16)
    grad_fc1 = jnp.einsum("nd,nf->df", normed_b, grad_pre, preferred_element_type=jnp.float32)
    grad_fc1_bias = jnp.sum(grad_pre, axis=0, dtype=jnp.float32)
    grad_normed_b = jnp.einsum(
        "nf,df->nd", grad_pre, first_feedforward_weight, preferred_element_type=jnp.float32
    )
    norm_value, norm_pull = jax.vjp(modulated, midway, shift_b, scale_b)
    grad_mid_norm, grad_shift_b, grad_scale_b = norm_pull(grad_normed_b)
    grad_midway = grad_rows + grad_mid_norm
    grad_branch = (gate_a * grad_midway).astype(jnp.bfloat16)
    grad_gate_a = jnp.sum(grad_midway * branch, axis=0)
    grad_proj = jnp.einsum("nc,nd->cd", attended, grad_branch, preferred_element_type=jnp.float32)
    grad_proj_bias = jnp.sum(grad_branch, axis=0, dtype=jnp.float32)
    grad_attended = jnp.einsum(
        "nd,cd->nc", grad_branch, output_projection_weight, preferred_element_type=jnp.float32
    )
    grad_attended = grad_attended.astype(jnp.bfloat16).reshape(query.shape)
    grad_query, grad_keys, grad_values = attend_back(
        query, key_heads, value_heads, log_total, grad_attended, temporal_layer_flag
    )
    grad_projected = jnp.stack([grad_query, grad_keys, grad_values], axis=2).reshape(
        row_count, 3 * features
    )
    grad_projected = grad_projected.astype(jnp.bfloat16)
    grad_qkv = jnp.einsum("nd,nq->dq", normed_a, grad_projected, preferred_element_type=jnp.float32)
    projected_sums = jnp.sum(grad_projected, axis=0, dtype=jnp.float32)
    grad_normed_a = jnp.einsum(
        "nq,dq->nd", grad_projected, query_key_value_weight, preferred_element_type=jnp.float32
    )
    norm_value, norm_pull = jax.vjp(modulated, token_rows, shift_a, scale_a)
    grad_tokens_norm, grad_shift_a, grad_scale_a = norm_pull(grad_normed_a)
    grad_tokens = grad_midway + grad_tokens_norm
    grad_mod = jnp.concatenate(
        [grad_shift_a, grad_scale_a, grad_gate_a, grad_shift_b, grad_scale_b, grad_gate_b]
    )
    bias_part = jnp.concatenate(
        [
            projected_sums[:features],
            projected_sums[2 * features :],
            grad_proj_bias,
            grad_fc1_bias,
            grad_fc2_bias,
        ]
    )
    return (
        grad_tokens.reshape(shape_in),
        grad_mod,
        (grad_qkv, grad_proj, grad_fc1, grad_fc2),
        bias_part,
    )


def fetch_forward(shards, layer_position_index):
    return (
        lax.all_gather(shards[0][layer_position_index], ("dat", "seq"), axis=0, tiled=True),
        lax.all_gather(shards[1][layer_position_index], ("dat", "seq"), axis=0, tiled=True),
        lax.all_gather(shards[2][layer_position_index], ("dat", "seq"), axis=0, tiled=True),
        lax.all_gather(shards[3][layer_position_index], ("dat", "seq"), axis=0, tiled=True),
        lax.all_gather(shards[4][layer_position_index], ("dat", "seq"), axis=0, tiled=True),
        lax.all_gather(shards[5][layer_position_index], ("dat", "seq"), axis=0, tiled=True),
    )


def fetch_backward(shards, layer_position_index):
    return (
        lax.all_gather(shards[0][layer_position_index], ("dat", "seq"), axis=0, tiled=True),
        lax.all_gather(shards[1][layer_position_index], ("dat", "seq"), axis=0, tiled=True),
        lax.all_gather(shards[2][layer_position_index], ("dat", "seq"), axis=0, tiled=True),
        lax.all_gather(shards[3][layer_position_index], ("dat", "seq"), axis=0, tiled=True),
        lax.all_gather(shards[4][layer_position_index], ("dat", "seq"), axis=0, tiled=True),
        lax.all_gather(shards[5][layer_position_index], ("dat", "seq"), axis=0, tiled=True),
    )


def per_device(
    clip_latents,
    conditioning,
    timesteps,
    clip_live,
    cotangent,
    ada_weight,
    query_key_value_weight,
    output_projection_weight,
    first_feedforward_weight,
    second_feedforward_weight,
    biases,
):
    layer_count = ada_weight.shape[0]
    features = clip_latents.shape[-1]
    first_flag = (lax.axis_index("seq") == 0).astype(jnp.float32)
    shards = (
        ada_weight,
        query_key_value_weight,
        output_projection_weight,
        first_feedforward_weight,
        second_feedforward_weight,
        biases,
    )
    summed = [
        [jnp.zeros(member.shape[1:], jnp.float32) for member in shards]
        for layer_position_index in range(layer_count)
    ]
    totals = [None for layer_position_index in range(layer_count)]
    out_list = []
    grad_list = []
    cond_list = []
    for slot_index in range(clip_latents.shape[0]):
        alive_flag = clip_live[slot_index].astype(jnp.float32)
        cond_total = conditioning[slot_index].astype(jnp.float32) + timestep_embed(
            timesteps[slot_index], features
        )
        cond_act = jax.nn.silu(cond_total).astype(jnp.bfloat16)
        latents = clip_latents[slot_index].astype(jnp.float32)
        residual_stream = latents
        fetched = []
        saved = []
        modulations = []
        for layer_position_index in range(layer_count):
            params = fetch_forward(shards, layer_position_index)
            adaptive_modulation = jnp.dot(
                cond_act[None, :], params[0], preferred_element_type=jnp.float32
            )[0]
            adaptive_modulation = adaptive_modulation + params[5][: 6 * features].astype(
                jnp.float32
            )
            temporal_layer_flag = layer_position_index % 2 == 1
            if temporal_layer_flag:
                residual_stream = lax.all_to_all(
                    residual_stream, "seq", split_axis=1, concat_axis=0, tiled=True
                )
            residual_stream, kept = layer_forward(
                residual_stream, adaptive_modulation, params, temporal_layer_flag
            )
            if temporal_layer_flag:
                residual_stream = lax.all_to_all(
                    residual_stream, "seq", split_axis=0, concat_axis=1, tiled=True
                )
            fetched.append(params)
            saved.append(kept)
            modulations.append(adaptive_modulation)
        out_list.append(jnp.where(alive_flag > 0, residual_stream, latents))
        cot_float = cotangent[slot_index].astype(jnp.float32)
        gradient = cot_float * alive_flag
        grad_cond_act = jnp.zeros((features,), jnp.float32)
        cond_float = cond_act.astype(jnp.float32)
        for layer_position_index in reversed(range(layer_count)):
            params = fetch_backward(shards, layer_position_index)
            temporal_layer_flag = layer_position_index % 2 == 1
            if temporal_layer_flag:
                gradient = lax.all_to_all(gradient, "seq", split_axis=1, concat_axis=0, tiled=True)
            gradient, grad_mod, matrices, bias_part = layer_backward(
                gradient,
                modulations[layer_position_index],
                params,
                saved[layer_position_index],
                temporal_layer_flag,
            )
            if temporal_layer_flag:
                gradient = lax.all_to_all(gradient, "seq", split_axis=0, concat_axis=1, tiled=True)
            mod_total = lax.psum(grad_mod, "seq")
            grad_cond_act = grad_cond_act + jnp.einsum(
                "m,dm->d", mod_total, params[0].astype(jnp.float32), precision=highest
            )
            grad_ada = jnp.einsum("d,m->dm", cond_float, mod_total, precision=highest) * first_flag
            grad_bias = jnp.concatenate([mod_total * first_flag, bias_part])
            terms = [grad_ada, matrices[0], matrices[1], matrices[2], matrices[3], grad_bias]
            if totals[layer_position_index] is None:
                totals[layer_position_index] = terms
            else:
                totals[layer_position_index] = [
                    running + new_term
                    for running, new_term in zip(totals[layer_position_index], terms)
                ]
        grad_list.append(jnp.where(alive_flag > 0, gradient, cot_float))
        silu_value, silu_pull = jax.vjp(jax.nn.silu, cond_total)
        cond_list.append(silu_pull(grad_cond_act)[0])
    for layer_position_index in range(layer_count):
        whole = totals[layer_position_index]
        shares = (
            lax.psum_scatter(whole[0], ("dat", "seq"), scatter_dimension=0, tiled=True),
            lax.psum_scatter(whole[1], ("dat", "seq"), scatter_dimension=0, tiled=True),
            lax.psum_scatter(whole[2], ("dat", "seq"), scatter_dimension=0, tiled=True),
            lax.psum_scatter(whole[3], ("dat", "seq"), scatter_dimension=0, tiled=True),
            lax.psum_scatter(whole[4], ("dat", "seq"), scatter_dimension=0, tiled=True),
            lax.psum_scatter(whole[5], ("dat", "seq"), scatter_dimension=0, tiled=True),
        )
        summed[layer_position_index] = list(shares)
    stacked = tuple(
        (
            jnp.stack(
                [
                    summed[layer_position_index][member_index]
                    for layer_position_index in range(layer_count)
                ]
            )
            for member_index in range(6)
        )
    )
    return (jnp.stack(out_list), jnp.stack(grad_list), jnp.stack(cond_list)) + stacked


def solution(mesh):
    in_specs = (
        P("dat", "seq", None, None),
        P("dat", None),
        P("dat"),
        P("dat"),
        P("dat", "seq", None, None),
        P(None, ("dat", "seq"), None),
        P(None, ("dat", "seq"), None),
        P(None, ("dat", "seq"), None),
        P(None, ("dat", "seq"), None),
        P(None, ("dat", "seq"), None),
        P(None, ("dat", "seq")),
    )
    out_specs = (
        P("dat", "seq", None, None),
        P("dat", "seq", None, None),
        P("dat", None),
        P(None, ("dat", "seq"), None),
        P(None, ("dat", "seq"), None),
        P(None, ("dat", "seq"), None),
        P(None, ("dat", "seq"), None),
        P(None, ("dat", "seq"), None),
        P(None, ("dat", "seq")),
    )
    return jax.shard_map(
        per_device, mesh=mesh, in_specs=in_specs, out_specs=out_specs, check_vma=False
    )
```

profile of v0, /device:TPU:8, one launch (start us, length us, event | category | flops | bytes accessed | tf_op | source)
XLA Modules:
  0.0 1181.4 jit_solution(15350972002738300085)
XLA Ops:
  19.2 3.7 all-to-all-start.4
  27.9 41.6 %all-reduce.22 = (bf16[5376]{0:T(1024)(128)(2,1)S(1)}, bf16[5376]{0:T(1024)(128)(2,1)S(1)}) all-reduce(bf16[5376]{0:T(1024)(128)(2,1)S(1)} %dynamic-update-slice, bf16[5376]{0:T(1024)(128)(2,1)S(1)} %dynamic-update-slice.1), channel_id=3, replica_groups=mesh['dat'=4,'seq'=8] {'dat','seq'}, use_global_device_ids=true, to_apply=%add | all-reduce | flops 10752 | bytes 43008
  70.9 35.8 %all-gather.9 = bf16[1,384,384]{2,0,1:T(2,128)(2,1)S(1)} all-gather(bf16[1,12,384]{2,0,1:T(2,128)(2,1)S(1)} %get-tuple-element.196), channel_id=11, replica_groups=mesh['dat'=4,'seq'=8] {'dat','seq'}, dimensions={1}, use_global_device_ids=true | all-gather | bytes 304128 | tf_op jit(solution)/shard_map/all_gather | solution.py:263
  106.7 41.3 %all-gather.3 = bf16[1,384,384]{2,0,1:T(2,128)(2,1)} all-gather(bf16[1,12,384]{2,0,1:T(2,128)(2,1)S(1)} %get-tuple-element.197), channel_id=5, replica_groups=mesh['dat'=4,'seq'=8] {'dat','seq'}, dimensions={1}, use_global_device_ids=true | all-gather | bytes 304128 | tf_op jit(solution)/shard_map/all_gather | solution.py:263
  148.0 49.1 %all-gather.8 = bf16[1,384,1152]{2,0,1:T(2,128)(2,1)} all-gather(bf16[1,12,1152]{2,0,1:T(2,128)(2,1)S(1)} %get-tuple-element.194), channel_id=10, replica_groups=mesh['dat'=4,'seq'=8] {'dat','seq'}, dimensions={1}, use_global_device_ids=true | all-gather | bytes 912384 | tf_op jit(solution)/shard_map/all_gather | solution.py:262
  199.2 46.7 %all-gather.2 = bf16[1,384,1152]{2,0,1:T(2,128)(2,1)} all-gather(bf16[1,12,1152]{2,0,1:T(2,128)(2,1)S(1)} %get-tuple-element.195), channel_id=4, replica_groups=mesh['dat'=4,'seq'=8] {'dat','seq'}, dimensions={1}, use_global_device_ids=true | all-gather | bytes 912384 | tf_op jit(solution)/shard_map/all_gather | solution.py:262
  246.0 3.8 all-to-all-start.6
  260.0 4.8 all-to-all-done.6
  281.5 2.9 reshape.707
  296.1 4.0 convolution_add_fusion.7
  300.1 24.9 %all-gather.23.cloned.1.call-done = bf16[1,1536,384]{2,1,0:T(8,128)(2,1)} async-done(((bf16[1,48,384]{2,1,0:T(8,128)(2,1)}), bf16[1,1536,384]{2,1,0:T(8,128)(2,1)}) %all-gather.23.cloned.1.call-update) | async-done | bytes 1179664 | tf_op jit(solution)/shard_map/all_gather | solution.py:265
  325.0 4.3 multiply_add_fusion.3
  330.8 4.7 all-to-all-start
  342.4 5.9 all-to-all-done
  354.7 3.0 fusion.37
  357.7 4.7 reshape.710
  375.4 3.5 convolution_add_fusion.6
  378.9 3.0 all-gather.29.cloned.1.call-done
  381.9 5.5 fusion.134
  387.5 3.4 convert_reduce_fusion.3
  401.3 3.5 multiply_reduce_fusion.5
  413.2 4.2 copy.227
  417.4 4.7 convert_element_type.480
  422.1 3.5 multiply_reduce_fusion.15
  427.2 4.4 all-to-all-start.5
  431.6 3.5 fusion.283
  439.3 4.9 all-to-all-done.5
  444.1 4.2 all-to-all-start.1
  449.7 5.7 convert_reduce_fusion.5
  484.4 4.4 all-to-all-start.2
  494.6 4.7 fusion.246
  507.8 3.0 fusion.39
  510.8 4.6 reshape.716
  531.9 3.2 convert_reduce_fusion.2
  543.7 3.5 multiply_reduce_fusion.4
  554.7 3.0 convolution_add_fusion.10
  563.2 4.7 convert_element_type.495
  567.9 3.5 multiply_reduce_fusion.10
  573.5 4.3 all-to-all-start.7
  577.9 3.9 convolution_add_fusion.8
  594.7 4.7 convolution_add_fusion.12
  599.5 4.2 all-to-all-start.3
  605.8 5.5 convert_reduce_fusion.4
  628.5 3.2 fusion.149
  651.8 27.0 %all-reduce.21 = (f32[2304]{0:T(1024)}, f32[2304]{0:T(1024)}, f32[2304]{0:T(1024)}, f32[2304]{0:T(1024)S(1)}) all-reduce(f32[2304]{0:T(1024)} %constant_dynamic-update-slice_fusion.10, f32[2304]{0:T(1024)} %copy-done.190, f32[2304]{0:T(1024)} %copy-done.192, ...), channel_id=1, replica_groups=mesh['dat'=4,'seq'=8] {'seq'}, use_global_device_ids=true, to_apply=%region_64.65 | all-reduce | flops 9216 | bytes 73728 | tf_op jit(solution)/shard_map/psum | solution.py:366
  692.7 226.7 %fusion.248 = (f32[16,2304]{1,0:T(8,128)}, f32[16,2304]{1,0:T(8,128)}, f32[16,1152]{1,0:T(8,128)}, f32[16,1152]{1,0:T(8,128)}, f32[16,384]{1,0:T(8,128)}, /*inde...) fusion(f32[384,2304]{1,0:T(8,128)} %get-tuple-element.239, f32[384,2304]{1,0:T(8,128)S(1)} %get-tuple-element.238, ...), kind=kCustom, calls=%all-reduce-scatter.8 | all-reduce-scatter fusion | flops 5505025 | bytes 17203200
  920.3 9.5 collective-permute-start.46
  929.8 6.6 collective-permute-start.45
  941.5 3.8 collective-permute-start.39
  952.0 4.8 convolution_add_fusion.11
  959.4 3.4 collective-permute-start.43
  964.8 3.1 collective-permute-start.41
  981.1 41.3 %all-reduce.20 = (f32[5376]{0:T(1024)S(1)}, f32[5376]{0:T(1024)S(1)}) all-reduce(f32[5376]{0:T(1024)S(1)} %add.683, f32[5376]{0:T(1024)S(1)} %add.682), channel_id=25, replica_groups=mesh['dat'=4,'seq'=8] {'dat','seq'}, use_global_device_ids=true, to_apply=%region_99.100.clone | all-reduce | flops 10752 | bytes 86016
  1022.6 4.1 collective-permute-start.33
  1028.7 4.8 collective-permute-start.30
  1065.2 3.4 collective-permute-start.17
  1083.9 3.1 collective-permute-start.58
  1119.7 2.9 concatenate.64
  1122.6 4.1 collective-permute-done.15
  1126.7 3.5 collective-permute-start.10
  1130.3 6.1 collective-permute-start.9
  1145.3 3.4 collective-permute-start.3
  1159.2 4.8 collective-permute-done.1
  1165.8 5.7 concatenate.58
  (1030 shorter events, 391.2 us)
Async XLA Ops:
  7.2 258.8 %all-gather.27.cloned.1.call-start = ((), (), s32[]{:S(2)}) async-start(), calls=%async_computation.16 | async-start | bytes 2433024 | tf_op jit(solution)/shard_map/all_gather | solution.py:264
  9.0 259.8 %all-gather.21.cloned.1.call-start = ((), (), s32[]{:S(2)}) async-start(), calls=%async_computation.13 | async-start | bytes 2433024 | tf_op jit(solution)/shard_map/all_gather | solution.py:264
  9.8 261.8 %all-gather.19.cloned.1.call-start = ((), (), s32[]{:S(2)}) async-start(), calls=%async_computation.12 | async-start | bytes 3649536 | tf_op jit(solution)/shard_map/all_gather | solution.py:261
  11.7 262.5 %all-gather.25.cloned.1.call-start = ((), (), s32[]{:S(2)}) async-start(), calls=%async_computation.15 | async-start | bytes 3649536 | tf_op jit(solution)/shard_map/all_gather | solution.py:261
  12.3 312.6 %all-gather.23.cloned.1.call-start = ((), (), s32[]{:S(2)}) async-start(), calls=%async_computation.14 | async-start | bytes 1216512 | tf_op jit(solution)/shard_map/all_gather | solution.py:265
  19.2 226.8 %all-to-all-start.4 = ((f32[2,256,384]{2,0,1:T(2,128)}), f32[2,256,384]{2,0,1:T(2,128)S(1)}, u32[]{:S(2)}, u32[]{:S(2)}) async-start(f32[2,256,384]{2,0,1:T(2,128)} %copy.222), calls=%async_computation.4 | async-start | bytes 1572864 | tf_op jit(solution)/shard_map/all_to_all | solution.py:356
  22.9 359.0 %all-gather.29.cloned.1.call-start = ((), (), s32[]{:S(2)}) async-start(), calls=%async_computation.17 | async-start | bytes 1216512 | tf_op jit(solution)/shard_map/all_gather | solution.py:265
  246.0 18.9 %all-to-all-start.6 = ((f32[2,256,384]{2,0,1:T(2,128)}), f32[2,256,384]{2,0,1:T(2,128)S(1)}, u32[]{:S(2)}, u32[]{:S(2)}) async-start(f32[2,256,384]{2,0,1:T(2,128)} %copy.236), calls=%async_computation.6 | async-start | bytes 1572864 | tf_op jit(solution)/shard_map/all_to_all | solution.py:356
  330.8 17.6 %all-to-all-start = ((f32[2,256,384]{2,0,1:T(2,128)}), f32[2,256,384]{2,0,1:T(2,128)}, u32[]{:S(2)}, u32[]{:S(2)}) async-start(f32[2,256,384]{2,0,1:T(2,128)} %copy.200), calls=%async_computation | async-start | bytes 1572864 | tf_op jit(solution)/shard_map/all_to_all | solution.py:334
  427.2 17.0 %all-to-all-start.5 = ((f32[16,32,384]{2,1,0:T(8,128)}), f32[16,32,384]{2,1,0:T(8,128)}, u32[]{:S(2)}, u32[]{:S(2)}) async-start(f32[16,32,384]{2,1,0:T(8,128)} %bitcast.603), calls=%async_computation.5 | async-start | bytes 1572864 | tf_op jit(solution)/shard_map/all_to_all | solution.py:365
  444.1 40.2 %all-to-all-start.1 = ((f32[16,32,384]{2,1,0:T(8,128)}), f32[16,32,384]{2,1,0:T(8,128)}, u32[]{:S(2)}, u32[]{:S(2)}) async-start(f32[16,32,384]{2,1,0:T(8,128)} %bitcast.614), calls=%async_computation.1 | async-start | bytes 1572864 | tf_op jit(solution)/shard_map/all_to_all | solution.py:341
  484.4 17.0 %all-to-all-start.2 = ((f32[2,256,384]{2,0,1:T(2,128)}), f32[2,256,384]{2,0,1:T(2,128)}, u32[]{:S(2)}, u32[]{:S(2)}) async-start(f32[2,256,384]{2,0,1:T(2,128)} %copy.214), calls=%async_computation.2 | async-start | bytes 1572864 | tf_op jit(solution)/shard_map/all_to_all | solution.py:334
  488.8 683.8 %reduce-scatter.21.cloned.1.call-start = ((), (), s32[]{:S(2)}) async-start(), calls=%async_computation.11 | async-start | bytes 2433024 | tf_op jit(solution)/shard_map/reduce_scatter | solution.py:390
  573.5 26.0 %all-to-all-start.7 = ((f32[16,32,384]{2,1,0:T(8,128)}), f32[16,32,384]{2,1,0:T(8,128)}, u32[]{:S(2)}, u32[]{:S(2)}) async-start(f32[16,32,384]{2,1,0:T(8,128)} %bitcast.602), calls=%async_computation.7 | async-start | bytes 1572864 | tf_op jit(solution)/shard_map/all_to_all | solution.py:365
  599.5 27.6 %all-to-all-start.3 = ((f32[16,32,384]{2,1,0:T(8,128)}), f32[16,32,384]{2,1,0:T(8,128)}, u32[]{:S(2)}, u32[]{:S(2)}) async-start(f32[16,32,384]{2,1,0:T(8,128)} %bitcast.615), calls=%async_computation.3 | async-start | bytes 1572864 | tf_op jit(solution)/shard_map/all_to_all | solution.py:341
  603.7 568.9 %reduce-scatter.19.cloned.1.call-start = ((), (), s32[]{:S(2)}) async-start(), calls=%async_computation.10 | async-start | bytes 2433024 | tf_op jit(solution)/shard_map/reduce_scatter | solution.py:390
  920.3 44.6 %collective-permute-start.46 = (f32[16,384]{1,0:T(8,128)}, f32[16,384]{1,0:T(8,128)S(1)}, u32[]{:S(2)}, u32[]{:S(2)}) collective-permute-start(f32[16,384]{1,0:T(8,128)} %get-tuple-element.106), channel_id=1, source_target_pairs={{0,7},{1,8},{2,9},{3,10},{4,11},{5,12},{6,13},{7,14},{8,15},{9,16}... | collective-permute-start | bytes 73736
  929.8 38.2 %collective-permute-start.45 = (f32[16,384]{1,0:T(8,128)}, f32[16,384]{1,0:T(8,128)S(1)}, u32[]{:S(2)}, u32[]{:S(2)}) collective-permute-start(f32[16,384]{1,0:T(8,128)} %get-tuple-element.106), channel_id=1, source_target_pairs={{0,6},{1,7},{2,8},{3,9},{4,10},{5,11},{6,12},{7,13},{8,14},{9,15},... | collective-permute-start | bytes 73736
  936.4 33.5 %collective-permute-start.44 = (f32[16,384]{1,0:T(8,128)}, f32[16,384]{1,0:T(8,128)S(1)}, u32[]{:S(2)}, u32[]{:S(2)}) collective-permute-start(f32[16,384]{1,0:T(8,128)} %get-tuple-element.106), channel_id=1, source_target_pairs={{0,5},{1,6},{2,7},{3,8},{4,9},{5,10},{6,11},{7,12},{8,13},{9,14},{... | collective-permute-start | bytes 73736
  941.5 17.9 %collective-permute-start.39 = (f32[12,384]{1,0:T(8,128)S(1)}, f32[12,384]{1,0:T(8,128)S(1)}, u32[]{:S(2)}, u32[]{:S(2)}) collective-permute-start(f32[12,384]{1,0:T(8,128)S(1)} %slice.340), channel_id=1, source_target_pairs={{0,8},{1,9},{2,10},{3,11},{4,12},{5,13},{6,14},{7,15},{8,16},{9,17... | collective-permute-start | bytes 55304
  945.4 17.5 %collective-permute-start.47 = (f32[12,384]{1,0:T(8,128)S(1)}, f32[12,384]{1,0:T(8,128)S(1)}, u32[]{:S(2)}, u32[]{:S(2)}) collective-permute-start(f32[12,384]{1,0:T(8,128)S(1)} %slice.341), channel_id=1, source_target_pairs={{0,8},{1,9},{2,10},{3,11},{4,12},{5,13},{6,14},{7,15},{8,16},{9,17... | collective-permute-start | bytes 55304
  959.4 13.0 %collective-permute-start.43 = (f32[16,384]{1,0:T(8,128)S(1)}, f32[16,384]{1,0:T(8,128)S(1)}, u32[]{:S(2)}, u32[]{:S(2)}) collective-permute-start(f32[16,384]{1,0:T(8,128)S(1)} %copy-done.124), channel_id=1, source_target_pairs={{0,4},{1,5},{2,6},{3,7},{4,8},{5,9},{6,10},{7,11},{8,12},{9,13},{1... | collective-permute-start | bytes 73736
  962.9 11.7 collective-permute-start.42
  964.8 12.0 %collective-permute-start.41 = (f32[16,384]{1,0:T(8,128)S(1)}, f32[16,384]{1,0:T(8,128)S(1)}, u32[]{:S(2)}, u32[]{:S(2)}) collective-permute-start(f32[16,384]{1,0:T(8,128)S(1)} %copy-done.124), channel_id=1, source_target_pairs={{0,2},{1,3},{2,4},{3,5},{4,6},{5,7},{6,8},{7,9},{8,10},{9,11},{10,... | collective-permute-start | bytes 73736
  969.9 52.7 %collective-permute-start.38 = (f32[16,384]{1,0:T(8,128)S(1)}, f32[16,384]{1,0:T(8,128)S(1)}, u32[]{:S(2)}, u32[]{:S(2)}) collective-permute-start(f32[16,384]{1,0:T(8,128)S(1)} %copy-done.123), channel_id=1, source_target_pairs={{0,7},{1,8},{2,9},{3,10},{4,11},{5,12},{6,13},{7,14},{8,15},{9,16}... | collective-permute-start | bytes 73736
  972.4 54.4 %collective-permute-start.37 = (f32[16,384]{1,0:T(8,128)S(1)}, f32[16,384]{1,0:T(8,128)S(1)}, u32[]{:S(2)}, u32[]{:S(2)}) collective-permute-start(f32[16,384]{1,0:T(8,128)S(1)} %copy-done.123), channel_id=1, source_target_pairs={{0,6},{1,7},{2,8},{3,9},{4,10},{5,11},{6,12},{7,13},{8,14},{9,15},... | collective-permute-start | bytes 73736
  974.6 54.1 %collective-permute-start.36 = (f32[16,384]{1,0:T(8,128)S(1)}, f32[16,384]{1,0:T(8,128)S(1)}, u32[]{:S(2)}, u32[]{:S(2)}) collective-permute-start(f32[16,384]{1,0:T(8,128)S(1)} %copy-done.123), channel_id=1, source_target_pairs={{0,5},{1,6},{2,7},{3,8},{4,9},{5,10},{6,11},{7,12},{8,13},{9,14},{... | collective-permute-start | bytes 73736
  976.8 56.7 %collective-permute-start.35 = (f32[16,384]{1,0:T(8,128)S(1)}, f32[16,384]{1,0:T(8,128)S(1)}, u32[]{:S(2)}, u32[]{:S(2)}) collective-permute-start(f32[16,384]{1,0:T(8,128)S(1)} %copy-done.123), channel_id=1, source_target_pairs={{0,4},{1,5},{2,6},{3,7},{4,8},{5,9},{6,10},{7,11},{8,12},{9,13},{1... | collective-permute-start | bytes 73736
  978.8 56.7 %collective-permute-start.34 = (f32[16,384]{1,0:T(8,128)S(1)}, f32[16,384]{1,0:T(8,128)S(1)}, u32[]{:S(2)}, u32[]{:S(2)}) collective-permute-start(f32[16,384]{1,0:T(8,128)S(1)} %copy-done.123), channel_id=1, source_target_pairs={{0,3},{1,4},{2,5},{3,6},{4,7},{5,8},{6,9},{7,10},{8,11},{9,12},{10... | collective-permute-start | bytes 73736
  1022.6 16.4 %collective-permute-start.33 = (f32[16,384]{1,0:T(8,128)S(1)}, f32[16,384]{1,0:T(8,128)S(1)}, u32[]{:S(2)}, u32[]{:S(2)}) collective-permute-start(f32[16,384]{1,0:T(8,128)S(1)} %copy-done.123), channel_id=1, source_target_pairs={{0,2},{1,3},{2,4},{3,5},{4,6},{5,7},{6,8},{7,9},{8,10},{9,11},{10,... | collective-permute-start | bytes 73736
  1026.8 14.2 %collective-permute-start.32 = (f32[16,384]{1,0:T(8,128)S(1)}, f32[16,384]{1,0:T(8,128)S(1)}, u32[]{:S(2)}, u32[]{:S(2)}) collective-permute-start(f32[16,384]{1,0:T(8,128)S(1)} %copy-done.123), channel_id=1, source_target_pairs={{0,1},{1,2},{2,3},{3,4},{4,5},{5,6},{6,7},{7,8},{8,9},{9,10},{10,1... | collective-permute-start | bytes 73736
  1028.7 20.9 %collective-permute-start.30 = (f32[16,1152]{1,0:T(8,128)S(1)}, f32[16,1152]{1,0:T(8,128)S(1)}, u32[]{:S(2)}, u32[]{:S(2)}) collective-permute-start(f32[16,1152]{1,0:T(8,128)S(1)} %copy-done.119), channel_id=1, source_target_pairs={{0,7},{1,8},{2,9},{3,10},{4,11},{5,12},{6,13},{7,14},{8,15},{9,16}... | collective-permute-start | bytes 221192
  1039.1 13.0 %collective-permute-start.29 = (f32[16,1152]{1,0:T(8,128)S(1)}, f32[16,1152]{1,0:T(8,128)S(1)}, u32[]{:S(2)}, u32[]{:S(2)}) collective-permute-start(f32[16,1152]{1,0:T(8,128)S(1)} %copy-done.119), channel_id=1, source_target_pairs={{0,6},{1,7},{2,8},{3,9},{4,10},{5,11},{6,12},{7,13},{8,14},{9,15},... | collective-permute-start | bytes 221192
  1041.0 13.0 %collective-permute-start.28 = (f32[16,1152]{1,0:T(8,128)S(1)}, f32[16,1152]{1,0:T(8,128)S(1)}, u32[]{:S(2)}, u32[]{:S(2)}) collective-permute-start(f32[16,1152]{1,0:T(8,128)S(1)} %copy-done.119), channel_id=1, source_target_pairs={{0,5},{1,6},{2,7},{3,8},{4,9},{5,10},{6,11},{7,12},{8,13},{9,14},{... | collective-permute-start | bytes 221192
  1044.8 11.7 collective-permute-start.27
  1047.1 11.7 collective-permute-start.26
  1049.6 11.7 collective-permute-start.25
  1056.6 12.0 %collective-permute-start.21 = (f32[16,1152]{1,0:T(8,128)S(1)}, f32[16,1152]{1,0:T(8,128)S(1)}, u32[]{:S(2)}, u32[]{:S(2)}) collective-permute-start(f32[16,1152]{1,0:T(8,128)S(1)} %copy-done.118), channel_id=1, source_target_pairs={{0,6},{1,7},{2,8},{3,9},{4,10},{5,11},{6,12},{7,13},{8,14},{9,15},... | collective-permute-start | bytes 221192
  1058.8 11.7 collective-permute-start.20
  1063.2 12.9 %collective-permute-start.18 = (f32[16,1152]{1,0:T(8,128)S(1)}, f32[16,1152]{1,0:T(8,128)S(1)}, u32[]{:S(2)}, u32[]{:S(2)}) collective-permute-start(f32[16,1152]{1,0:T(8,128)S(1)} %copy-done.118), channel_id=1, source_target_pairs={{0,3},{1,4},{2,5},{3,6},{4,7},{5,8},{6,9},{7,10},{8,11},{9,12},{10... | collective-permute-start | bytes 221192
  1065.2 12.9 %collective-permute-start.17 = (f32[16,1152]{1,0:T(8,128)S(1)}, f32[16,1152]{1,0:T(8,128)S(1)}, u32[]{:S(2)}, u32[]{:S(2)}) collective-permute-start(f32[16,1152]{1,0:T(8,128)S(1)} %copy-done.118), channel_id=1, source_target_pairs={{0,2},{1,3},{2,4},{3,5},{4,6},{5,7},{6,8},{7,9},{8,10},{9,11},{10,... | collective-permute-start | bytes 221192
  1076.2 12.0 %collective-permute-start.62 = (f32[16,1536]{1,0:T(8,128)S(1)}, f32[16,1536]{1,0:T(8,128)S(1)}, u32[]{:S(2)}, u32[]{:S(2)}) collective-permute-start(f32[16,1536]{1,0:T(8,128)S(1)} %copy-done.110), channel_id=1, source_target_pairs={{0,7},{1,8},{2,9},{3,10},{4,11},{5,12},{6,13},{7,14},{8,15},{9,16}... | collective-permute-start | bytes 294920
  1078.1 12.0 %collective-permute-start.61 = (f32[16,1536]{1,0:T(8,128)S(1)}, f32[16,1536]{1,0:T(8,128)S(1)}, u32[]{:S(2)}, u32[]{:S(2)}) collective-permute-start(f32[16,1536]{1,0:T(8,128)S(1)} %copy-done.110), channel_id=1, source_target_pairs={{0,6},{1,7},{2,8},{3,9},{4,10},{5,11},{6,12},{7,13},{8,14},{9,15},... | collective-permute-start | bytes 294920
  1080.0 12.2 %collective-permute-start.60 = (f32[16,1536]{1,0:T(8,128)S(1)}, f32[16,1536]{1,0:T(8,128)S(1)}, u32[]{:S(2)}, u32[]{:S(2)}) collective-permute-start(f32[16,1536]{1,0:T(8,128)S(1)} %copy-done.110), channel_id=1, source_target_pairs={{0,5},{1,6},{2,7},{3,8},{4,9},{5,10},{6,11},{7,12},{8,13},{9,14},{... | collective-permute-start | bytes 294920
  1082.0 12.2 %collective-permute-start.59 = (f32[16,1536]{1,0:T(8,128)S(1)}, f32[16,1536]{1,0:T(8,128)S(1)}, u32[]{:S(2)}, u32[]{:S(2)}) collective-permute-start(f32[16,1536]{1,0:T(8,128)S(1)} %copy-done.110), channel_id=1, source_target_pairs={{0,4},{1,5},{2,6},{3,7},{4,8},{5,9},{6,10},{7,11},{8,12},{9,13},{1... | collective-permute-start | bytes 294920
  1083.9 12.2 %collective-permute-start.58 = (f32[16,1536]{1,0:T(8,128)S(1)}, f32[16,1536]{1,0:T(8,128)S(1)}, u32[]{:S(2)}, u32[]{:S(2)}) collective-permute-start(f32[16,1536]{1,0:T(8,128)S(1)} %copy-done.110), channel_id=1, source_target_pairs={{0,3},{1,4},{2,5},{3,6},{4,7},{5,8},{6,9},{7,10},{8,11},{9,12},{10... | collective-permute-start | bytes 294920
  1098.1 11.9 %collective-permute-start.51 = (f32[16,1536]{1,0:T(8,128)S(1)}, f32[16,1536]{1,0:T(8,128)S(1)}, u32[]{:S(2)}, u32[]{:S(2)}) collective-permute-start(f32[16,1536]{1,0:T(8,128)S(1)} %copy-done.109), channel_id=1, source_target_pairs={{0,4},{1,5},{2,6},{3,7},{4,8},{5,9},{6,10},{7,11},{8,12},{9,13},{1... | collective-permute-start | bytes 294920
  1100.0 11.9 %collective-permute-start.50 = (f32[16,1536]{1,0:T(8,128)S(1)}, f32[16,1536]{1,0:T(8,128)S(1)}, u32[]{:S(2)}, u32[]{:S(2)}) collective-permute-start(f32[16,1536]{1,0:T(8,128)S(1)} %copy-done.109), channel_id=1, source_target_pairs={{0,3},{1,4},{2,5},{3,6},{4,7},{5,8},{6,9},{7,10},{8,11},{9,12},{10... | collective-permute-start | bytes 294920
  1101.9 11.9 %collective-permute-start.49 = (f32[16,1536]{1,0:T(8,128)S(1)}, f32[16,1536]{1,0:T(8,128)}, u32[]{:S(2)}, u32[]{:S(2)}) collective-permute-start(f32[16,1536]{1,0:T(8,128)S(1)} %copy-done.109), channel_id=1, source_target_pairs={{0,2},{1,3},{2,4},{3,5},{4,6},{5,7},{6,8},{7,9},{8,10},{9,11},{10,... | collective-permute-start | bytes 294920
  1104.1 11.7 collective-permute-start.48
  1106.1 11.7 collective-permute-start.7
  1110.0 20.3 %collective-permute-start.14 = (f32[16,2304]{1,0:T(8,128)S(1)}, f32[16,2304]{1,0:T(8,128)S(1)}, u32[]{:S(2)}, u32[]{:S(2)}) collective-permute-start(f32[16,2304]{1,0:T(8,128)S(1)} %copy-done.102), channel_id=1, source_target_pairs={{0,7},{1,8},{2,9},{3,10},{4,11},{5,12},{6,13},{7,14},{8,15},{9,16}... | collective-permute-start | bytes 442376
  1111.9 24.4 %collective-permute-start.13 = (f32[16,2304]{1,0:T(8,128)S(1)}, f32[16,2304]{1,0:T(8,128)S(1)}, u32[]{:S(2)}, u32[]{:S(2)}) collective-permute-start(f32[16,2304]{1,0:T(8,128)S(1)} %copy-done.102), channel_id=1, source_target_pairs={{0,6},{1,7},{2,8},{3,9},{4,10},{5,11},{6,12},{7,13},{8,14},{9,15},... | collective-permute-start | bytes 442376
  1113.8 24.9 %collective-permute-start.12 = (f32[16,2304]{1,0:T(8,128)S(1)}, f32[16,2304]{1,0:T(8,128)S(1)}, u32[]{:S(2)}, u32[]{:S(2)}) collective-permute-start(f32[16,2304]{1,0:T(8,128)S(1)} %copy-done.102), channel_id=1, source_target_pairs={{0,5},{1,6},{2,7},{3,8},{4,9},{5,10},{6,11},{7,12},{8,13},{9,14},{... | collective-permute-start | bytes 442376
  1115.8 25.1 %collective-permute-start.11 = (f32[16,2304]{1,0:T(8,128)S(1)}, f32[16,2304]{1,0:T(8,128)S(1)}, u32[]{:S(2)}, u32[]{:S(2)}) collective-permute-start(f32[16,2304]{1,0:T(8,128)S(1)} %copy-done.102), channel_id=1, source_target_pairs={{0,4},{1,5},{2,6},{3,7},{4,8},{5,9},{6,10},{7,11},{8,12},{9,13},{1... | collective-permute-start | bytes 442376
  1126.7 16.1 %collective-permute-start.10 = (f32[16,2304]{1,0:T(8,128)S(1)}, f32[16,2304]{1,0:T(8,128)S(1)}, u32[]{:S(2)}, u32[]{:S(2)}) collective-permute-start(f32[16,2304]{1,0:T(8,128)S(1)} %copy-done.102), channel_id=1, source_target_pairs={{0,3},{1,4},{2,5},{3,6},{4,7},{5,8},{6,9},{7,10},{8,11},{9,12},{10... | collective-permute-start | bytes 442376
  1130.3 15.0 %collective-permute-start.9 = (f32[16,2304]{1,0:T(8,128)S(1)}, f32[16,2304]{1,0:T(8,128)S(1)}, u32[]{:S(2)}, u32[]{:S(2)}) collective-permute-start(f32[16,2304]{1,0:T(8,128)S(1)} %copy-done.102), channel_id=1, source_target_pairs={{0,2},{1,3},{2,4},{3,5},{4,6},{5,7},{6,8},{7,9},{8,10},{9,11},{10,... | collective-permute-start | bytes 442376
  1136.4 12.3 %collective-permute-start.8 = (f32[16,2304]{1,0:T(8,128)S(1)}, f32[16,2304]{1,0:T(8,128)S(1)}, u32[]{:S(2)}, u32[]{:S(2)}) collective-permute-start(f32[16,2304]{1,0:T(8,128)S(1)} %copy-done.102), channel_id=1, source_target_pairs={{0,1},{1,2},{2,3},{3,4},{4,5},{5,6},{6,7},{7,8},{8,9},{9,10},{10,1... | collective-permute-start | bytes 442376
  1138.8 11.8 %collective-permute-start.6 = (f32[16,2304]{1,0:T(8,128)S(1)}, f32[16,2304]{1,0:T(8,128)S(1)}, u32[]{:S(2)}, u32[]{:S(2)}) collective-permute-start(f32[16,2304]{1,0:T(8,128)S(1)} %copy-done.101), channel_id=1, source_target_pairs={{0,7},{1,8},{2,9},{3,10},{4,11},{5,12},{6,13},{7,14},{8,15},{9,16}... | collective-permute-start | bytes 442376
  1140.9 11.8 collective-permute-start.5
  1142.9 14.0 %collective-permute-start.4 = (f32[16,2304]{1,0:T(8,128)S(1)}, f32[16,2304]{1,0:T(8,128)}, u32[]{:S(2)}, u32[]{:S(2)}) collective-permute-start(f32[16,2304]{1,0:T(8,128)S(1)} %copy-done.101), channel_id=1, source_target_pairs={{0,5},{1,6},{2,7},{3,8},{4,9},{5,10},{6,11},{7,12},{8,13},{9,14},{... | collective-permute-start | bytes 442376
  1145.3 12.2 %collective-permute-start.3 = (f32[16,2304]{1,0:T(8,128)S(1)}, f32[16,2304]{1,0:T(8,128)}, u32[]{:S(2)}, u32[]{:S(2)}) collective-permute-start(f32[16,2304]{1,0:T(8,128)S(1)} %copy-done.101), channel_id=1, source_target_pairs={{0,4},{1,5},{2,6},{3,7},{4,8},{5,9},{6,10},{7,11},{8,12},{9,13},{1... | collective-permute-start | bytes 442376
  1150.6 13.3 %collective-permute-start.1 = (f32[16,2304]{1,0:T(8,128)S(1)}, f32[16,2304]{1,0:T(8,128)}, u32[]{:S(2)}, u32[]{:S(2)}) collective-permute-start(f32[16,2304]{1,0:T(8,128)S(1)} %copy-done.101), channel_id=1, source_target_pairs={{0,2},{1,3},{2,4},{3,5},{4,6},{5,7},{6,8},{7,9},{8,10},{9,11},{10,... | collective-permute-start | bytes 442376
  1152.7 13.2 %collective-permute-start = (f32[16,2304]{1,0:T(8,128)S(1)}, f32[16,2304]{1,0:T(8,128)}, u32[]{:S(2)}, u32[]{:S(2)}) collective-permute-start(f32[16,2304]{1,0:T(8,128)S(1)} %copy-done.101), channel_id=1, source_target_pairs={{0,1},{1,2},{2,3},{3,4},{4,5},{5,6},{6,7},{7,8},{8,9},{9,10},{10,1... | collective-permute-start | bytes 442376
  (284 other events, 3211.8 us)
Sparse Core Ops, SparseCore 0:
  11.5 57.4 all-gather.26
  72.5 57.1 all-gather.20
  133.2 64.9 all-gather.18
  201.5 63.5 all-gather.24
  267.9 57.0 all-gather.22
  328.3 53.5 all-gather.28
  557.8 105.8 reduce-scatter.20
  956.9 97.9 reduce-scatter.18
where the time goes:
time: 1190 us; the launch traced here: 1180 us
  blocking collectives  509 us (43%)
  starting transfers between devices  196 us (16%)
  matrix products  164 us (14%)
  local copies, waits for them, and re-layouts  163 us (14%)
  other arithmetic  66.5 us (6%)
  waiting for transfers between devices  60.6 us (5%)
  between operations  22.1 us (2%)
    unnamed x3, blocking collectives  310 us
    unnamed x64, starting transfers between devices  162 us
    all_gather x2, blocking collectives, fetch_forward(): lax.all_gather(shards[1][layer_position_index], ('dat', 'seq'), axis=0, t...  95.8 us
    all_gather x2, blocking collectives, fetch_forward(): lax.all_gather(shards[2][layer_position_index], ('dat', 'seq'), axis=0, t...  77.1 us
    unnamed x616, local copies, waits for them, and re-layouts  59.3 us
    all_gather x2, waiting for transfers between devices, fetch_forward(): lax.all_gather(shards[4][layer_position_index], ('dat', 'seq'), axis=0, t...  27.8 us
    psum x1, blocking collectives, per_device(): mod_total = lax.psum(grad_mod, 'seq')  27 us
  transfers between devices with their start and end apart: 80, of which 11 were waited for; matrix products, arithmetic and copies ran while one was open for 43% of the time, Pallas kernels for 0%

commit v1 on v0

v1 whole, which is shorter than its diff:
```python
from functools import partial
import math

import jax
import jax.numpy as jnp
from jax import lax
from jax.experimental import pallas as pl
from jax.experimental.pallas import tpu as pltpu
from jax.sharding import PartitionSpec as P

H = 6
HD = 64
EPS = 1e-06
BF = jnp.bfloat16
F32 = jnp.float32
GELU_A = math.sqrt(2.0 / math.pi)
GELU_B = 0.044715
VMEM_LIMIT = 60 * 1024 * 1024


def dot_nn(a, b):
    return lax.dot_general(a, b, (((1,), (0,)), ((), ())), preferred_element_type=F32)


def dot_nt(a, b):
    return lax.dot_general(a, b, (((1,), (1,)), ((), ())), preferred_element_type=F32)


def dot_tn(a, b):
    return lax.dot_general(a, b, (((0,), (0,)), ((), ())), preferred_element_type=F32)


def normalize(v):
    center = v - jnp.mean(v, axis=-1, keepdims=True)
    rstd = lax.rsqrt(jnp.mean(center * center, axis=-1, keepdims=True) + EPS)
    return center * rstd, rstd


def normalize_back(grad, normed, rstd):
    m1 = jnp.mean(grad, axis=-1, keepdims=True)
    m2 = jnp.mean(grad * normed, axis=-1, keepdims=True)
    return rstd * (grad - m1 - normed * m2)


def column_sum(v):
    return jnp.sum(v.astype(F32), axis=0, keepdims=True)


def gelu_parts(v):
    sq = v * v
    th = jnp.tanh(v * (GELU_A + (GELU_A * GELU_B) * sq))
    half = 0.5 + 0.5 * th
    act = v * half
    slope = half + act * (1.0 - th) * (GELU_A + (3.0 * GELU_A * GELU_B) * sq)
    return act, slope


def head_masks(rows):
    lane = lax.broadcasted_iota(jnp.int32, (rows, 2 * HD), 1)
    return lane < HD, lane >= HD


def pick(mask, v):
    return jnp.where(mask, v, jnp.zeros_like(v))


def attend_tile(projected, width, group, place_mask):
    rows = projected.shape[0]
    masks = head_masks(group)
    scale = 1.0 / math.sqrt(HD)
    blocks, totals = [], []
    for g in range(rows // group):
        part = projected[g * group : (g + 1) * group]
        pairs = []
        for j in range(width // (2 * HD)):
            at = 2 * HD * j
            q2 = part[:, at : at + 2 * HD]
            k2 = part[:, width + at : width + at + 2 * HD]
            v2 = part[:, 2 * width + at : 2 * width + at + 2 * HD]
            out = None
            for mask in masks:
                s = dot_nt(k2, pick(mask, q2)) * scale
                if place_mask is not None:
                    s = jnp.where(place_mask, s, -1e30)
                peak = jnp.max(s, axis=0, keepdims=True)
                e = jnp.exp(s - peak)
                total = jnp.sum(e, axis=0, keepdims=True)
                totals.append(peak + jnp.log(total))
                p = (e * (1.0 / total)).astype(BF)
                term = dot_tn(p, pick(mask, v2))
                out = term if out is None else out + term
            pairs.append(out)
        blocks.append(jnp.concatenate(pairs, axis=1))
    return jnp.concatenate(blocks, axis=0), totals


def attend_back_tile(projected, totals, grad_attended, width, group, place_mask):
    rows = projected.shape[0]
    masks = head_masks(group)
    scale = 1.0 / math.sqrt(HD)
    blocks = []
    index = 0
    for g in range(rows // group):
        part = projected[g * group : (g + 1) * group]
        ga = grad_attended[g * group : (g + 1) * group]
        dqs, dks, dvs = [], [], []
        for j in range(width // (2 * HD)):
            at = 2 * HD * j
            q2 = part[:, at : at + 2 * HD]
            k2 = part[:, width + at : width + at + 2 * HD]
            v2 = part[:, 2 * width + at : 2 * width + at + 2 * HD]
            do2 = ga[:, at : at + 2 * HD]
            dq = dk = dv = None
            for mask in masks:
                qm, dom, km = pick(mask, q2), pick(mask, do2), pick(mask, k2)
                p = jnp.exp(dot_nt(k2, qm) * scale - totals[index])
                if place_mask is not None:
                    p = jnp.where(place_mask, p, 0.0)
                index += 1
                dp = dot_nt(v2, dom)
                rowdot = jnp.sum(dp * p, axis=0, keepdims=True)
                ds = (p * (dp - rowdot)).astype(BF)
                tv = dot_nn(p.astype(BF), dom)
                tk = dot_nn(ds, qm)
                tq = dot_tn(ds, km)
                dv = tv if dv is None else dv + tv
                dk = tk if dk is None else dk + tk
                dq = tq if dq is None else dq + tq
            dqs.append((dq * scale).astype(BF))
            dks.append((dk * scale).astype(BF))
            dvs.append(dv.astype(BF))
        blocks.append(jnp.concatenate(dqs + dks + dvs, axis=1))
    return jnp.concatenate(blocks, axis=0)


def forward_tile(x, mod, bias, weights, group, place_mask):
    wqkv, wo, w1, w2 = weights
    d = x.shape[-1]
    sh_a, sc_a, g_a, sh_b, sc_b, g_b = [mod[i : i + 1] for i in range(6)]
    na, rstd_a = normalize(x)
    normed_a = (na * (1.0 + sc_a) + sh_a).astype(BF)
    projected = (dot_nn(normed_a, wqkv[...]) + bias[:, : 3 * d]).astype(BF)
    attended, totals = attend_tile(projected, d, group, place_mask)
    attended = attended.astype(BF)
    branch = dot_nn(attended, wo[...]) + bias[:, 3 * d : 4 * d]
    step_a = g_a * branch
    mid = x + step_a
    nb, rstd_b = normalize(mid)
    normed_b = (nb * (1.0 + sc_b) + sh_b).astype(BF)
    act, slope = gelu_parts(dot_nn(normed_b, w1[...]) + bias[:, 4 * d : -d])
    act = act.astype(BF)
    slope = slope.astype(BF)
    mlp = dot_nn(act, w2[...]) + bias[:, -d:]
    delta = step_a + g_b * mlp
    kept = dict(
        na=na, rstd_a=rstd_a, mid=mid, normed_a=normed_a, projected=projected, totals=totals,
        attended=attended, branch=branch, nb=nb, rstd_b=rstd_b, normed_b=normed_b,
        act=act, slope=slope, mlp=mlp,
    )
    return delta, kept


def backward_tile(g, mod, kept, weights, sums, group, place_mask):
    wqkv, wo, w1, w2 = weights
    aqkv, ao, a1, a2 = sums
    d = g.shape[-1]
    sh_a, sc_a, g_a, sh_b, sc_b, g_b = [mod[i : i + 1] for i in range(6)]
    gm = (g_b * g).astype(BF)
    t_gate_b = jnp.sum(g * kept["mlp"].astype(F32), axis=0, keepdims=True)
    a2[...] += dot_tn(kept["act"], gm)
    gp = (dot_nt(gm, w2[...]) * kept["slope"].astype(F32)).astype(BF)
    a1[...] += dot_tn(kept["normed_b"], gp)
    gnb = dot_nt(gp, w1[...])
    t_shift_b = jnp.sum(gnb, axis=0, keepdims=True)
    t_scale_b = jnp.sum(gnb * kept["nb"], axis=0, keepdims=True)
    dmid = normalize_back((1.0 + sc_b) * gnb, kept["nb"], kept["rstd_b"])
    gmid = g + dmid
    gbr = (g_a * gmid).astype(BF)
    t_gate_a = jnp.sum(gmid * kept["branch"].astype(F32), axis=0, keepdims=True)
    ao[...] += dot_tn(kept["attended"], gbr)
    ga = dot_nt(gbr, wo[...]).astype(BF)
    gproj = attend_back_tile(kept["projected"], kept["totals"], ga, d, group, place_mask)
    aqkv[...] += dot_tn(kept["normed_a"], gproj)
    gna = dot_nt(gproj, wqkv[...])
    t_shift_a = jnp.sum(gna, axis=0, keepdims=True)
    t_scale_a = jnp.sum(gna * kept["na"], axis=0, keepdims=True)
    dx = dmid + normalize_back((1.0 + sc_a) * gna, kept["na"], kept["rstd_a"])
    mods = [t_shift_a, t_scale_a, t_gate_a, t_shift_b, t_scale_b, t_gate_b]
    biases = [column_sum(gproj), column_sum(gbr), column_sum(gp), column_sum(gm)]
    return dx, mods, jnp.concatenate(biases, axis=1)


def unpack_weights(owner, row_map, parts, weights):
    wqkv, wo, w1, w2 = weights
    d = wo.shape[0]
    n_rows = row_map.shape[1]
    line = lax.broadcasted_iota(jnp.int32, (d, n_rows), 0)
    place = [(line == row_map[i : i + 1, :]).astype(F32).astype(BF) for i in range(4)]

    def columns(at):
        return jnp.concatenate(
            [p[:, :, at : at + d].reshape(-1, d) for p in parts], axis=0
        )

    blocks = [columns(d * c) for c in range(6)]
    wqkv[:, :d] = dot_nn(place[0], blocks[0]).astype(BF)
    for c in range(4):
        w1[:, d * c : d * (c + 1)] = dot_nn(place[0], blocks[1 + c]).astype(BF)
    wo[...] = dot_nn(place[0], blocks[5]).astype(BF)
    for half in range(2):
        total = None
        for t in range(3):
            term = dot_nn(place[1 + t], blocks[2 * t + half])
            total = term if total is None else total + term
        wqkv[:, d * (1 + half) : d * (2 + half)] = total.astype(BF)
    at = 0
    for p in parts:
        for k in range(p.shape[0]):
            base = pl.multiple_of(owner[at + k] * 48, 16)
            for t in range(3):
                w2[pl.ds(base + 16 * t, 16), :] = p[k, :, 6 * d + d * t : 6 * d + d * (t + 1)]
        at += p.shape[0]


def pack_terms(owner, column_map, sums, out):
    aqkv, ao, a1, a2 = sums
    d = ao.shape[0]
    n_rows = column_map.shape[0]
    lane = lax.broadcasted_iota(jnp.int32, (n_rows, d), 1)
    place = [(lane == column_map[:, i : i + 1]).astype(F32).astype(BF) for i in range(4)]
    main = [aqkv[:, :d]] + [a1[:, d * c : d * (c + 1)] for c in range(4)] + [ao[...]]
    rest = [aqkv[:, d * (1 + half) : d * (2 + half)].astype(BF) for half in range(2)]
    for c in range(6):
        block = dot_nn(place[0], main[c].astype(BF)) + dot_nn(place[1 + c // 2], rest[c % 2])
        out[:, :, d * c : d * (c + 1)] = block.astype(BF).reshape(-1, 16, d)
    for k in range(out.shape[0]):
        base = pl.multiple_of(owner[k] * 48, 16)
        for t in range(3):
            out[k, :, 6 * d + d * t : 6 * d + d * (t + 1)] = a2[pl.ds(base + 16 * t, 16), :].astype(BF)


def spatial_forward_kernel(n_parts, owner, row_map, *refs):
    parts, refs = refs[:n_parts], refs[n_parts:]
    x_ref, mod_ref, bias_ref = refs[:3]
    weights = refs[3:7]
    (send, stream, totals, normed_a, projected, attended, branch, mid, normed_b, act,
     slope, mlp) = refs[7:]

    @pl.when(pl.program_id(0) == 0)
    def _():
        unpack_weights(owner, row_map, parts, weights)

    x = x_ref[0, 0].astype(F32)
    delta, kept = forward_tile(x, mod_ref[0], bias_ref[...], weights, x.shape[0], None)
    total = x + delta
    stream[0, 0] = total
    send[...] = total.astype(BF).reshape(send.shape)
    totals[0] = jnp.concatenate(kept["totals"] + [jnp.zeros_like(kept["totals"][0])] * 2, axis=0)
    normed_a[...] = kept["normed_a"]
    projected[...] = kept["projected"]
    attended[...] = kept["attended"]
    branch[...] = kept["branch"].astype(BF)
    mid[...] = kept["mid"]
    normed_b[...] = kept["normed_b"]
    act[...] = kept["act"]
    slope[...] = kept["slope"]
    mlp[...] = kept["mlp"].astype(BF)


def clear(step, refs):
    @pl.when(step)
    def _():
        for r in refs:
            r[...] = jnp.zeros_like(r)


def add_rows(ref, rows, first):
    block = jnp.concatenate(rows + [jnp.zeros_like(rows[0])] * 2, axis=0)
    clear(first, [ref])
    ref[0] += block


def gather_rows(block):
    frames = block.shape[0] * block.shape[2]
    v = block.astype(F32).reshape(frames, block.shape[3], block.shape[4])
    groups = [
        v[:, 8 * b : 8 * (b + 1)].reshape(8 * frames, v.shape[2]) for b in range(v.shape[1] // 8)
    ]
    return jnp.concatenate(groups, axis=0)


def scatter_rows(rows, shape):
    frames = shape[0] * shape[2]
    groups = [
        rows[8 * frames * b : 8 * frames * (b + 1)].reshape(frames, 8, shape[4])
        for b in range(shape[3] // 8)
    ]
    return jnp.concatenate(groups, axis=1).astype(BF).reshape(shape)


def temporal_kernel(n_parts, per_clip, owner, row_map, column_map, *refs):
    parts, refs = refs[:n_parts], refs[n_parts:]
    x_ref, g_ref, mod_ref, bias_ref = refs[:4]
    out_delta, grad_delta, mods, biases, payload = refs[4:9]
    weights, sums = refs[9:13], refs[13:17]
    step = pl.program_id(0)

    @pl.when(step == 0)
    def _():
        unpack_weights(owner, row_map, parts, weights)

    clear(step == 0, list(sums) + [biases])
    x = gather_rows(x_ref[...])
    g = gather_rows(g_ref[...])
    group = 8 * x_ref.shape[0] * x_ref.shape[2]
    row = lax.broadcasted_iota(jnp.int32, (group, group), 0)
    lane = lax.broadcasted_iota(jnp.int32, (group, group), 1)
    place_mask = ((row ^ lane) & 7) == 0
    mod = mod_ref[0]
    delta, kept = forward_tile(x, mod, bias_ref[...], weights, group, place_mask)
    out_delta[...] = scatter_rows(delta, out_delta.shape)
    dx, mod_rows, bias_row = backward_tile(g, mod, kept, weights, sums, group, place_mask)
    grad_delta[...] = scatter_rows(dx, grad_delta.shape)
    add_rows(mods, mod_rows, step % per_clip == 0)
    biases[...] += bias_row

    @pl.when(step == pl.num_programs(0) - 1)
    def _():
        pack_terms(owner, column_map, sums, payload)


def spatial_backward_kernel(per_clip, owner, live, column_map, *refs):
    x_ref, cot_ref, gd_ref, mod_ref = refs[:4]
    weights = refs[4:8]
    totals, normed_a, projected, attended, branch, mid, normed_b, act, slope, mlp = refs[8:18]
    grad_out, mods, biases, payload = refs[18:22]
    sums = refs[22:26]
    step = pl.program_id(0)
    clear(step == 0, list(sums) + [biases])
    alive = live[step // per_clip].astype(F32)
    cot = cot_ref[0, 0].astype(F32)
    g = cot * alive + gd_ref[...].astype(F32).reshape(cot.shape)
    mod = mod_ref[0]
    na, rstd_a = normalize(x_ref[0, 0].astype(F32))
    nb, rstd_b = normalize(mid[...])
    kept = dict(
        na=na, rstd_a=rstd_a, nb=nb, rstd_b=rstd_b, normed_a=normed_a[...],
        projected=projected[...], totals=[totals[0, h : h + 1] for h in range(H)],
        attended=attended[...], branch=branch[...], normed_b=normed_b[...],
        act=act[...], slope=slope[...], mlp=mlp[...],
    )
    dx, mod_rows, bias_row = backward_tile(g, mod, kept, weights, sums, cot.shape[0], None)
    grad_out[0, 0] = jnp.where(alive > 0, g + dx, cot)
    add_rows(mods, mod_rows, step % per_clip == 0)
    biases[...] += bias_row

    @pl.when(step == pl.num_programs(0) - 1)
    def _():
        pack_terms(owner, column_map, sums, payload)


def whole(a):
    zeros = (0,) * len(a.shape)
    return pl.BlockSpec(a.shape, lambda t: zeros, pipeline_mode=pl.Buffered(1))


def smem():
    return pl.BlockSpec(memory_space=pltpu.SMEM)


def shape(dims, dtype):
    return jax.ShapeDtypeStruct(dims, dtype)


PARAMS = pltpu.CompilerParams(
    dimension_semantics=("arbitrary",), vmem_limit_bytes=VMEM_LIMIT
)


def weight_shapes(d, ff, make):
    return [make((d, 3 * d)), make((d, d)), make((d, ff)), make((ff, d))]


def spatial_forward(owner, row_map, parts, x, mod, bias):
    clips, frames, places, d = x.shape
    ff = bias.shape[1] - 5 * d
    dests = lax.axis_size("seq")
    tiles = clips * frames
    rows = tiles * places
    tile4 = pl.BlockSpec((1, 1, places, d), lambda t: (t // frames, t % frames, 0, 0))

    def row_block(cols):
        return pl.BlockSpec((places, cols), lambda t: (t, 0))

    outs = [shape((d, 3 * d), BF), shape((d, d), BF), shape((d, ff), BF), shape((ff, d), BF)]
    specs = [whole(o) for o in outs]
    outs += [shape((dests, clips, frames, places // dests, d), BF), shape(x.shape, F32),
             shape((tiles, 8, places), F32)]
    specs += [
        pl.BlockSpec((dests, 1, 1, places // dests, d), lambda t: (0, t // frames, t % frames, 0, 0)),
        tile4, pl.BlockSpec((1, 8, places), lambda t: (t, 0, 0)),
    ]
    for cols, dtype in ((d, BF), (3 * d, BF), (d, BF), (d, BF), (d, F32), (d, BF), (ff, BF), (ff, BF), (d, BF)):
        outs.append(shape((rows, cols), dtype))
        specs.append(row_block(cols))
    return pl.pallas_call(
        partial(spatial_forward_kernel, len(parts)),
        grid=(tiles,),
        in_specs=[smem(), whole(row_map)] + [whole(p) for p in parts]
        + [tile4, pl.BlockSpec((1, 8, d), lambda t: (t // frames, 0, 0)), whole(bias)],
        out_specs=specs,
        out_shape=outs,
        compiler_params=PARAMS,
        name="spatial_forward",
    )(owner, row_map, *parts, x, mod, bias)


def temporal_block(owner, row_map, column_map, parts, x, g, mod, bias):
    sources, clips, frames, places, d = x.shape
    ff = bias.shape[1] - 5 * d
    span = 16
    per_clip = places // span
    tile = pl.BlockSpec(
        (sources, 1, frames, span, d), lambda t: (0, t // per_clip, 0, t % per_clip, 0)
    )
    mod_spec = pl.BlockSpec((1, 8, d), lambda t: (t // per_clip, 0, 0))
    n = owner.shape[0]
    outs = [shape(x.shape, BF), shape(x.shape, BF), shape((clips, 8, d), F32),
            shape(bias.shape, F32), shape((n, 16, 9 * d), BF)]
    return pl.pallas_call(
        partial(temporal_kernel, len(parts), per_clip),
        grid=(clips * per_clip,),
        in_specs=[smem(), whole(row_map), whole(column_map)] + [whole(p) for p in parts]
        + [tile, tile, mod_spec, whole(bias)],
        out_specs=[tile, tile, mod_spec, whole(bias), whole(outs[4])],
        out_shape=outs,
        scratch_shapes=weight_shapes(d, ff, lambda s: pltpu.VMEM(s, BF))
        + weight_shapes(d, ff, lambda s: pltpu.VMEM(s, F32)),
        compiler_params=PARAMS,
        name="temporal_block",
    )(owner, row_map, column_map, *parts, x, g, mod, bias)


def spatial_backward(owner, live, column_map, x, cot, grad_delta, mod, weights, saved):
    clips, frames, places, d = x.shape
    ff = weights[3].shape[0]
    dests = grad_delta.shape[0]
    tile4 = pl.BlockSpec((1, 1, places, d), lambda t: (t // frames, t % frames, 0, 0))
    mod_spec = pl.BlockSpec((1, 8, d), lambda t: (t // frames, 0, 0))
    n = owner.shape[0]
    outs = [shape(x.shape, F32), shape((clips, 8, d), F32), shape((1, 5 * d + ff), F32),
            shape((n, 16, 9 * d), BF)]
    return pl.pallas_call(
        partial(spatial_backward_kernel, frames),
        grid=(clips * frames,),
        in_specs=[smem(), smem(), whole(column_map), tile4, tile4,
                  pl.BlockSpec((dests, 1, 1, places // dests, d), lambda t: (0, t // frames, t % frames, 0, 0)),
                  mod_spec] + [whole(w) for w in weights]
        + [pl.BlockSpec((1, 8, places), lambda t: (t, 0, 0))]
        + [pl.BlockSpec((places, s.shape[1]), lambda t: (t, 0)) for s in saved[1:]],
        out_specs=[tile4, mod_spec, whole(outs[2]), whole(outs[3])],
        out_shape=outs,
        scratch_shapes=weight_shapes(d, ff, lambda s: pltpu.VMEM(s, F32)),
        compiler_params=PARAMS,
        name="spatial_backward",
    )(owner, live, column_map, x, cot, grad_delta, mod, *weights, *saved)


def row_maps(owner):
    i = jnp.arange(16, dtype=jnp.int32)[None, :]
    base = 12 * owner[:, None]
    cols = [jnp.where(i < 12, base + i, -1)]
    for t in range(3):
        cols.append(jnp.where(i >= 12, base + 4 * t + i - 12, -1))
    rows = jnp.stack([c.reshape(-1) for c in cols] + [jnp.full((16 * owner.shape[0],), -1, jnp.int32)] * 4)
    return rows, rows.T


def pack_shard(qkv, proj, fc1, fc2):
    d = proj.shape[1]
    main = jnp.concatenate([qkv[:, :d], fc1, proj], axis=1)
    rest = jnp.concatenate([qkv[4 * t : 4 * t + 4, d:] for t in range(3)], axis=1)
    tail = jnp.concatenate([fc2[16 * t : 16 * t + 16] for t in range(3)], axis=1)
    return jnp.concatenate([jnp.concatenate([main, rest], axis=0), tail], axis=1)


def unpack_shard(packed):
    d = packed.shape[1] // 9
    rest = [packed[12:, 2 * d * t : 2 * d * (t + 1)] for t in range(3)]
    qkv = jnp.concatenate([packed[:12, :d], jnp.concatenate(rest, axis=0)], axis=1)
    fc2 = jnp.concatenate([packed[:, 6 * d + d * t : 6 * d + d * (t + 1)] for t in range(3)], axis=0)
    return qkv, packed[:12, 5 * d : 6 * d], packed[:12, d : 5 * d], fc2


AXES = ("dat", "seq")


def swap(v, distance_of):
    pairs = [(i, i ^ distance_of(i)) for i in range(lax.axis_size("dat") * lax.axis_size("seq"))]
    return lax.ppermute(v, AXES, pairs)


def first_hop(i):
    return 4 if i % 2 else 2


def second_hop(i):
    return 2 if i % 2 else 4


def core_hop(i):
    return 1


def exchange(v, axis):
    return lax.all_to_all(v, axis, split_axis=0, concat_axis=0, tiled=True)


def spread(v, axis, size):
    return exchange(jnp.broadcast_to(v[None], (size,) + v.shape), axis)


def chain_owner(dat, me):
    core = me % 2
    p3 = jnp.where(core == 1, 4, 2)
    p4 = jnp.where(core == 1, 2, 4)
    q = me ^ 1
    low = jnp.stack([me, me ^ p3, me ^ p4, me ^ p3 ^ p4, q, q ^ p4, q ^ p3, q ^ p3 ^ p4])
    return (low[:, None] + 8 * jnp.arange(dat)[None, :]).reshape(-1).astype(jnp.int32)


def chain_gather(shard, dat):
    a = spread(shard, "dat", dat)
    b = swap(a, first_hop)
    ab = jnp.concatenate([a, b])
    e1 = swap(ab, core_hop)
    c = swap(ab, second_hop)
    e2 = swap(c, core_hop)
    return [ab, c, e1, e2]


def chain_reduce(payload, dat):
    half = payload.shape[0] // 2

    def step(v, hop):
        m = v.shape[0] // 2
        return (v[:m].astype(F32) + swap(v[m:], hop).astype(F32)).astype(BF)

    v = step(payload, core_hop)
    v = step(v, second_hop)
    v = step(v, first_hop)
    return jnp.sum(exchange(v, "dat").astype(F32), axis=0)


def whole_shards(weights):
    gathered = [lax.all_gather(w, AXES, axis=0, tiled=True) for w in weights]
    count = gathered[0].shape[0] // 12
    return jnp.stack([
        pack_shard(*[w[size * k : size * (k + 1)] for w, size in zip(gathered, (12, 12, 12, 48))])
        for k in range(count)
    ])


def scatter_whole(payload):
    cut = [unpack_shard(payload[k].astype(F32)) for k in range(payload.shape[0])]
    joined = [jnp.concatenate([c[i] for c in cut]) for i in range(4)]
    return [lax.psum_scatter(w, AXES, scatter_dimension=0, tiled=True) for w in joined]


def timestep_embed(timestep, features):
    half_count = features // 2
    frequency = jnp.exp(-math.log(10000.0) * jnp.arange(half_count, dtype=F32) / half_count)
    angles = timestep.astype(F32)[:, None] * frequency
    return jnp.concatenate([jnp.cos(angles), jnp.sin(angles)], axis=1)


def per_device(latents, conditioning, timesteps, live, cotangent, ada, qkv, proj, fc1, fc2, biases):
    dat, seq = lax.axis_size("dat"), lax.axis_size("seq")
    n = dat * seq
    group, place = lax.axis_index("dat"), lax.axis_index("seq")
    index = group * seq + place
    layers, own, wide = ada.shape
    clips, frames, places, d = latents.shape
    fast = dat == 4 and seq == 8 and own == 12
    share = biases.shape[1]
    total_bias = share * n
    part = layers * wide // seq
    highest = lax.Precision.HIGHEST

    alive = live.astype(BF)[:, None, None, None]
    cot_send = (cotangent * alive).reshape(clips, frames, seq, places // seq, d).transpose(2, 0, 1, 3, 4)
    cot_places = exchange(cot_send, "seq")

    if fast:
        shards = [pack_shard(qkv[l], proj[l], fc1[l], fc2[l]) for l in range(layers)]
        parts0 = chain_gather(shards[0], dat)
        owner0 = chain_owner(dat, place)
        parts1 = [lax.all_gather(shards[1], AXES, axis=0)]
        owner1 = jnp.arange(n, dtype=jnp.int32)
    else:
        parts0, parts1 = [[whole_shards([w[l] for w in (qkv, proj, fc1, fc2)])] for l in range(2)]
        owner0 = owner1 = jnp.arange(parts0[0].shape[0], dtype=jnp.int32)
    rows0, cols0 = row_maps(owner0)
    rows1, cols1 = row_maps(owner1)

    cond_total = conditioning.astype(F32) + timestep_embed(timesteps, d)
    cond_act = jax.nn.silu(cond_total).astype(BF)
    cond_all = spread(cond_act, "dat", dat).reshape(dat * clips, d)
    cond_mine = lax.dynamic_slice(cond_all, (0, index * own), (dat * clips, own))
    terms = jnp.einsum("cd,ldm->clm", cond_mine, ada, preferred_element_type=F32)
    terms = terms.reshape(dat, clips, seq, part).transpose(0, 2, 1, 3).reshape(n, clips * part)
    bias_sent = jnp.broadcast_to(biases.astype(F32).reshape(1, layers * share), (n, layers * share))
    got = exchange(jnp.concatenate([terms, bias_sent], axis=1), AXES)
    mod_part = jnp.sum(got[:, : clips * part], axis=0)
    bias_rows = got[:, clips * part :].reshape(n, layers, share).transpose(1, 0, 2).reshape(layers, total_bias)
    mod_all = spread(mod_part, "seq", seq).reshape(seq, clips, part).transpose(1, 0, 2)
    mod_all = mod_all.reshape(clips, layers, wide) + bias_rows[None, :, :wide]
    mod_all = jnp.pad(mod_all.reshape(clips, layers, 6, d), ((0, 0), (0, 0), (0, 2), (0, 0)))
    bias_all = jnp.concatenate(
        [bias_rows[:, wide : wide + d], jnp.zeros((layers, d), F32), bias_rows[:, wide + d :]], axis=1
    )

    outs = spatial_forward(owner0, rows0, parts0, latents, mod_all[:, 0], bias_all[:1])
    weights0, sent, stream, saved = outs[:4], outs[4], outs[5], outs[6:]
    stream_places = exchange(sent, "seq")
    out_delta, grad_delta, mods1, sums1, payload1 = temporal_block(
        owner1, rows1, cols1, parts1, stream_places, cot_places, mod_all[:, 1], bias_all[1:]
    )
    grad_back = exchange(grad_delta, "seq")
    out_back = exchange(out_delta, "seq")
    grad_latents, mods0, sums0, payload0 = spatial_backward(
        owner0, live, cols0, latents, cotangent, grad_back, mod_all[:, 0], weights0, saved
    )
    delta = out_back.transpose(1, 2, 0, 3, 4).reshape(latents.shape).astype(F32)
    out_latents = jnp.where((live > 0)[:, None, None, None], stream + delta, latents.astype(F32))

    if fast:
        flat = payload1.reshape(n * 16, payload1.shape[2])
        share1 = lax.psum_scatter(flat, AXES, scatter_dimension=0, tiled=True).astype(F32)
        share0 = chain_reduce(payload0, dat)
        shares = [unpack_shard(share0), unpack_shard(share1)]
    else:
        shares = [scatter_whole(payload0), scatter_whole(payload1)]
    grads = [jnp.stack([shares[l][i] for l in range(layers)]) for i in range(4)]

    mods = jnp.stack([mods0[:, :6], mods1[:, :6]], axis=1).reshape(clips, seq, part)
    mod_sum = jnp.sum(exchange(mods.transpose(1, 0, 2), "seq"), axis=0)
    sums = jnp.concatenate([sums0, sums1])
    bias_terms = jnp.concatenate(
        [jnp.sum(mods, axis=0).reshape(layers, wide), sums[:, :d], sums[:, 2 * d :]], axis=1
    )
    bias_terms = bias_terms.reshape(layers, n, share).transpose(1, 0, 2).reshape(n, layers * share)
    mod_sent = jnp.broadcast_to(mod_sum.reshape(1, clips * part), (n, clips * part))
    got = exchange(jnp.concatenate([mod_sent, bias_terms], axis=1), AXES)
    grad_biases = jnp.sum(got[:, clips * part :], axis=0).reshape(layers, share)
    mod_total = got[:, : clips * part].reshape(dat, seq, clips, part).transpose(0, 2, 1, 3)
    mod_total = mod_total.reshape(dat * clips, layers, wide)
    grad_ada = jnp.einsum("cd,clm->ldm", cond_mine.astype(F32), mod_total, precision=highest)
    cond_terms = jnp.einsum("clm,ldm->cd", mod_total, ada.astype(F32), precision=highest)
    cond_sent = jnp.broadcast_to(
        cond_terms.reshape(dat, 1, clips, own), (dat, seq, clips, own)
    ).reshape(n, clips, own)
    grad_cond = exchange(cond_sent, AXES).transpose(1, 0, 2).reshape(clips, d)
    grad_conditioning = jax.vjp(jax.nn.silu, cond_total)[1](grad_cond)[0]
    return (out_latents, grad_latents, grad_conditioning, grad_ada, *grads, grad_biases)


def solution(mesh):
    rows = P(None, ("dat", "seq"), None)
    tokens = P("dat", "seq", None, None)
    in_specs = (tokens, P("dat", None), P("dat"), P("dat"), tokens, rows, rows, rows, rows, rows,
                P(None, ("dat", "seq")))
    out_specs = (tokens, tokens, P("dat", None), rows, rows, rows, rows, rows, P(None, ("dat", "seq")))
    return jax.shard_map(
        per_device, mesh=mesh, in_specs=in_specs, out_specs=out_specs, check_vma=False
    )
```

time: 1190 us -> 362 us (0.30)
  blocking collectives: 509 us -> 0 us
  matrix products: 164 us -> 2.73 us
  starting transfers between devices: 196 us -> 56.4 us
  local copies, waits for them, and re-layouts: 163 us -> 39.5 us
  Pallas kernels: 0 us -> 107 us
  waiting for transfers between devices: 60.6 us -> 117 us
  other arithmetic: 66.5 us -> 18.4 us
    unnamed x3 -> x0, blocking collectives: 310 us -> none
    all_gather x4 -> x0, blocking collectives: 173 us -> none  [the longest x2 95.8 us: fetch_forward(): lax.all_gather(shards[1][layer_position_index], ('dat', 'seq'), axis=0, t...]
    unnamed x64 -> x0, starting transfers between devices: 162 us -> none
    dot_general x80 -> x3, matrix products: 164 us -> 2.73 us  [the longest x1 1.43 us: per_device(): jnp.einsum('clm,ldm->cd', mod_total, ada.astype(F32), precision=highest)]
    pallas_call x0 -> x3, Pallas kernels: none -> 107 us  [the longest x1 56.2 us: temporal_block(): pl.pallas_call(partial(temporal_kernel, len(parts), per_clip), grid=(clip...]
    unnamed x616 -> x80, local copies, waits for them, and re-layouts: 59.3 us -> 8.53 us
    all_to_all x8 -> x12, waiting for transfers between devices: 17.7 us -> 66.7 us  [exchange(): return lax.all_to_all(v, axis, split_axis=0, concat_axis=0, tiled=True)]
    convert_element_type x16 -> x1, local copies, waits for them, and re-layouts: 33.7 us -> 0.12 us  [per_device(): delta = out_back.transpose(1, 2, 0, 3, 4).reshape(latents.shape).astype(F32)]
  transfers between devices with their start and end apart: 80 -> 21, of which waited for: 11 -> 12; matrix products, arithmetic and copies ran while one was open for 43% -> 12% of each run, Pallas kernels for 0% -> 6%
where the time goes in v1:
time: 362 us; the launch traced here: 356 us
  waiting for transfers between devices  117 us (32%)
  Pallas kernels  107 us (30%)
  starting transfers between devices  56.4 us (16%)
  local copies, waits for them, and re-layouts  39.5 us (11%)
  other arithmetic  18.4 us (5%)
  between operations  15.1 us (4%)
    all_to_all x12, waiting for transfers between devices, exchange(): return lax.all_to_all(v, axis, split_axis=0, concat_axis=0, tiled=True)  66.7 us
    pallas_call x1, Pallas kernels, temporal_block(): pl.pallas_call(partial(temporal_kernel, len(parts), per_clip), grid=(clip...  56.2 us
    all_to_all x12, starting transfers between devices, exchange(): return lax.all_to_all(v, axis, split_axis=0, concat_axis=0, tiled=True)  48.9 us
    pallas_call x1, Pallas kernels, spatial_backward(): pl.pallas_call(partial(spatial_backward_kernel, frames), grid=(clips * fr...  28.7 us
    reduce_scatter x1, waiting for transfers between devices, per_device(): lax.psum_scatter(flat, AXES, scatter_dimension=0, tiled=True).astype(F32)  26.3 us
    ppermute x7, waiting for transfers between devices, swap(): return lax.ppermute(v, AXES, pairs)  23.7 us
    pallas_call x1, Pallas kernels, spatial_forward(): pl.pallas_call(partial(spatial_forward_kernel, len(parts)), grid=(tiles,)...  22.2 us
    unnamed x80, local copies, waits for them, and re-layouts  8.53 us
  transfers between devices with their start and end apart: 21, of which 12 were waited for; matrix products, arithmetic and copies ran while one was open for 12% of the time, Pallas kernels for 6%

profile of v1, /device:TPU:8, one launch (start us, length us, event | category | flops | bytes accessed | tf_op | source)
XLA Modules:
  0.0 356.0 jit_solution(12005806513103774337)
XLA Ops:
  7.2 1.0 fusion.25
  8.3 0.8 slice_bitcast_fusion.8
  9.1 1.1 fusion.24
  10.2 0.8 fusion.29
  13.9 5.3 %all-to-all-start.1 = ((bf16[4,2,384]{2,1,0:T(2,128)(2,1)}), bf16[4,2,384]{2,1,0:T(2,128)(2,1)S(1)}, u32[]{:S(2)}, u32[]{:S(2)}) async-start(bf16[4,2,384]{2,1,0:T(2,128)(2,1)} %broadcast_in_dim.120), calls=%async_computation.1 | async-start | bytes 12288 | tf_op jit(solution)/shard_map/all_to_all | solution.py:516
  20.4 3.0 all-to-all-done.1
  24.8 0.9 copy.105
  25.7 4.0 %all-to-all-start.2 = ((f32[32,1,1488]{2,1,0:T(1,128)}), f32[32,1,1488]{2,1,0:T(1,128)S(1)}, u32[]{:S(2)}, u32[]{:S(2)}) async-start(f32[32,1,1488]{2,1,0:T(1,128)} %copy.105), calls=%async_computation.2 | async-start | bytes 393216 | tf_op jit(solution)/shard_map/all_to_all | solution.py:516
  29.7 8.5 %all-to-all-done.2 = f32[32,1,1488]{2,1,0:T(1,128)S(1)} async-done(((f32[32,1,1488]{2,1,0:T(1,128)}), f32[32,1,1488]{2,1,0:T(1,128)S(1)}, u32[]{:S(2)}, u32[]{:S(2)}) %all-to-all-start.2) | async-done | bytes 190496 | tf_op jit(solution)/shard_map/all_to_all | solution.py:516
  38.2 0.8 broadcast_in_dim.119
  39.0 4.5 %all-to-all-start = ((bf16[4,16,3456]{2,1,0:T(8,128)(2,1)}), bf16[4,16,3456]{2,1,0:T(8,128)(2,1)S(1)}, u32[]{:S(2)}, u32[]{:S(2)}) async-start(bf16[4,16,3456]{2,1,0:T(8,128)(2,1)} %broadcast_in_dim.119), calls=%async_computation | async-start | bytes 884736 | tf_op jit(solution)/shard_map/all_to_all | solution.py:516
  44.7 1.0 copy.159
  47.3 8.9 %all-to-all-done = bf16[4,16,3456]{2,1,0:T(8,128)(2,1)S(1)} async-done(((bf16[4,16,3456]{2,1,0:T(8,128)(2,1)}), bf16[4,16,3456]{2,1,0:T(8,128)(2,1)S(1)}, u32[]{:S(2)}, u32[]{:S(2)}) %all-to-all-start) | async-done | bytes 442400 | tf_op jit(solution)/shard_map/all_to_all | solution.py:516
  56.9 3.3 all-to-all-start.3
  60.2 1.9 collective-permute-start
  62.2 12.2 %collective-permute-done = bf16[4,16,3456]{2,1,0:T(8,128)(2,1)S(1)} collective-permute-done((bf16[4,16,3456]{2,1,0:T(8,128)(2,1)S(1)}, bf16[4,16,3456]{2,1,0:T(8,128)(2,1)S(1)}, u32[]{:S(2)}, u32[]{:S(2)}) %collective-permute-start) | collective-permute-done | bytes 442400 | tf_op jit(solution)/shard_map/ppermute | solution.py:500
  74.5 1.5 collective-permute-start.1
  76.1 11.5 %collective-permute-done.1.refs_1_ = bf16[8,16,3456]{2,1,0:T(8,128)(2,1)S(1)} collective-permute-done((bf16[8,16,3456]{2,1,0:T(8,128)(2,1)S(1)}, bf16[8,16,3456]{2,1,0:T(8,128)(2,1)S(1)}, u32[]{:S(2)}, u32[]{:S(2)}) %collective-permute-start.1) | collective-permute-done | bytes 884768 | tf_op jit(solution)/shard_map/ppermute | solution.py:500
  87.6 3.6 all-to-all-start.5
  93.8 0.9 reshape.484
  95.5 0.9 copy-done.7
  96.4 22.2 %spatial_forward.1 = (bf16[384,1152]{1,0:T(8,128)(2,1)}, bf16[384,384]{1,0:T(8,128)(2,1)}, bf16[384,1536]{1,0:T(8,128)(2,1)}, bf16[1536,384]{1,0:T(8,128)(2,1)},...) custom-call(s32[32]{0:T(128)} %copy-done.30, ...), custom_call_target="tpu_custom_call" | custom-call | tf_op jit(solution)/shard_map/spatial_forward/pallas_call | solution.py:406
  118.6 4.1 %all-to-all-start.4 = ((bf16[8,2,2,32,384]{4,3,2,1,0:T(8,128)(2,1)}), bf16[8,2,2,32,384]{4,3,2,1,0:T(8,128)(2,1)S(1)}, u32[]{:S(2)}, u32[]{:S(2)}) async-start(bf16[8,2,2,32,384]{4,3,2,1,0:T(8,128)(2,1)} %get-tuple-element.35), calls=%async_computation.4 | async-start | bytes 1572864 | tf_op jit(solution)/shard_map/all_to_all | solution.py:516
  123.2 0.8 copy.109
  124.0 11.4 %all-to-all-done.4.refs_1_ = bf16[8,2,2,32,384]{4,3,2,1,0:T(8,128)(2,1)S(1)} async-done(((bf16[8,2,2,32,384]{4,3,2,1,0:T(8,128)(2,1)}), bf16[8,2,2,32,384]{4,3,2,1,0:T(8,128)(2,1)S(1)}, u32[]{:S(2)}, u32[]{:S(2)}) %all-to-all-start.4) | async-done | bytes 786464 | tf_op jit(solution)/shard_map/all_to_all | solution.py:516
  136.3 56.2 %temporal_block.1 = (bf16[8,2,2,32,384]{4,3,2,1,0:T(8,128)(2,1)}, bf16[8,2,2,32,384]{4,3,2,1,0:T(8,128)(2,1)}, f32[2,8,384]{2,1,0:T(8,128)}, f32[1,3456]{1,0:T(1,128)}, bf16[32,16,3456]{2,1,0:T(8,128)(2,1)}) custom-call(s32[32]{0:T(128)} %iota.59.owner, s32[8,512]{1,0:T(8,128)} %copy-done.13, s32[512,8]{1,0:T(8,128)} %bitcast.115, ...), custom_call_target="tpu_custom_call" | custom-call | tf_op jit(solution)/shard_map/temporal_block/pallas_call | solution.py:430
  192.4 3.6 all-to-all-start.7
  196.1 0.8 copy.115
  196.9 11.6 %all-to-all-done.7.refs_2_ = bf16[8,2,2,32,384]{4,3,2,1,0:T(8,128)(2,1)S(1)} async-done(((bf16[8,2,2,32,384]{4,3,2,1,0:T(8,128)(2,1)}), bf16[8,2,2,32,384]{4,3,2,1,0:T(8,128)(2,1)S(1)}, u32[]{:S(2)}, u32[]{:S(2)}) %all-to-all-start.7) | async-done | bytes 786464 | tf_op jit(solution)/shard_map/all_to_all | solution.py:516
  208.5 0.9 copy-done.2
  209.4 28.7 %spatial_backward.1 = (f32[2,2,256,384]{3,2,1,0:T(8,128)}, f32[2,8,384]{2,1,0:T(8,128)}, f32[1,3456]{1,0:T(1,128)}, bf16[32,16,3456]{2,1,0:T(8,128)(2,1)}) custom-call(s32[32]{0:T(128)} %copy-done.30, s32[2]{0:T(128)} %live.1, s32[512,8]{1,0:T(8,128)} %bitcast.114, bf16[2,2,256,384]{3,2,1,0:T(8,128)(2,1)} %refs_0_.1, bf16[2,2,256,384]{3,2,1,0:T(8,128)(2,1)} %refs_1_.1, ...), custom_call_target="tpu_custom_call" | custom-call | tf_op jit(solution)/shard_map/spatial_backward/pallas_call | solution.py:453
  238.2 1.6 slice.245
  242.0 4.0 %all-to-all-start.8 = ((f32[8,2,576]{2,1,0:T(2,128)}), f32[8,2,576]{2,1,0:T(2,128)}, u32[]{:S(2)}, u32[]{:S(2)}) async-start(f32[8,2,576]{2,1,0:T(2,128)} %copy.117), calls=%async_computation.8 | async-start | bytes 81920 | tf_op jit(solution)/shard_map/all_to_all | solution.py:516
  246.0 2.5 add_convert_fusion
  248.6 2.0 collective-permute-start.5
  251.2 1.5 reshape.491
  252.7 1.5 copy.162
  254.3 1.6 reshape.492
  255.8 4.2 %all-to-all-start.6 = ((bf16[8,2,2,32,384]{4,3,2,1,0:T(8,128)(2,1)}), bf16[8,2,2,32,384]{4,3,2,1,0:T(8,128)(2,1)}, u32[]{:S(2)}, u32[]{:S(2)}) async-start(bf16[8,2,2,32,384]{4,3,2,1,0:T(8,128)(2,1)} %get-tuple-element.36), calls=%async_computation.6 | async-start | bytes 1572864 | tf_op jit(solution)/shard_map/all_to_all | solution.py:516
  260.1 0.8 reduce_sum.46
  261.0 0.8 pad_maximum_fusion
  261.8 0.8 all_to_all.58
  262.8 0.8 slice.288
  263.6 1.9 collective-permute-start.6
  265.5 7.3 %all-to-all-done.6 = bf16[8,2,2,32,384]{4,3,2,1,0:T(8,128)(2,1)} async-done(((bf16[8,2,2,32,384]{4,3,2,1,0:T(8,128)(2,1)}), bf16[8,2,2,32,384]{4,3,2,1,0:T(8,128)(2,1)}, u32[]{:S(2)}, u32[]{:S(2)}) %all-to-all-start.6) | async-done | bytes 786464 | tf_op jit(solution)/shard_map/all_to_all | solution.py:516
  272.8 4.0 %all-to-all-start.9 = ((f32[32,1,1488]{2,1,0:T(1,128)}), f32[32,1,1488]{2,1,0:T(1,128)S(1)}, u32[]{:S(2)}, u32[]{:S(2)}) async-start(f32[32,1,1488]{2,1,0:T(1,128)} %all_to_all.58), calls=%async_computation.9 | async-start | bytes 393216 | tf_op jit(solution)/shard_map/all_to_all | solution.py:516
  276.8 1.3 convert_bitcast_fusion
  278.3 6.6 %all-to-all-done.9 = f32[32,1,1488]{2,1,0:T(1,128)S(1)} async-done(((f32[32,1,1488]{2,1,0:T(1,128)}), f32[32,1,1488]{2,1,0:T(1,128)S(1)}, u32[]{:S(2)}, u32[]{:S(2)}) %all-to-all-start.9) | async-done | bytes 190496 | tf_op jit(solution)/shard_map/all_to_all | solution.py:516
  285.6 0.8 reshape.493
  286.5 0.9 copy.119
  287.4 0.8 reshape.494
  288.2 1.4 convolution_bitcast_fusion.1
  290.3 3.4 all-to-all-start.10
  293.7 1.9 add_convert_fusion.2
  295.6 4.2 %all-to-all-done.10 = f32[32,2,12]{2,1,0:T(2,128)S(1)} async-done(((f32[32,2,12]{2,1,0:T(2,128)}), f32[32,2,12]{2,1,0:T(2,128)S(1)}, u32[]{:S(2)}, u32[]{:S(2)}) %all-to-all-start.10) | async-done | bytes 3104 | tf_op jit(solution)/shard_map/all_to_all | solution.py:516
  299.9 4.9 %all-to-all-start.11 = ((bf16[4,16,3456]{2,1,0:T(8,128)(2,1)}), bf16[4,16,3456]{2,1,0:T(8,128)(2,1)S(1)}, u32[]{:S(2)}, u32[]{:S(2)}) async-start(bf16[4,16,3456]{2,1,0:T(8,128)(2,1)} %add_convert_fusion.2), calls=%async_computation.11 | async-start | bytes 884736 | tf_op jit(solution)/shard_map/all_to_all | solution.py:516
  304.7 2.9 fusion
  307.8 1.1 convolution_bitcast_fusion
  308.9 0.9 copy.126
  309.8 0.8 slice_reduce_fusion.1
  312.1 5.0 %all-to-all-done.11 = bf16[4,16,3456]{2,1,0:T(8,128)(2,1)S(1)} async-done(((bf16[4,16,3456]{2,1,0:T(8,128)(2,1)}), bf16[4,16,3456]{2,1,0:T(8,128)(2,1)S(1)}, u32[]{:S(2)}, u32[]{:S(2)}) %all-to-all-start.11) | async-done | bytes 442400 | tf_op jit(solution)/shard_map/all_to_all | solution.py:516
  317.3 26.3 %reduce-scatter.2.cloned.1.call-done = bf16[16,3456]{1,0:T(8,128)(2,1)} async-done(((bf16[512,3456]{1,0:T(8,128)(2,1)}), bf16[16,3456]{1,0:T(8,128)(2,1)}) %reduce-scatter.2.cloned.1.call-update) | async-done | bytes 110608 | tf_op jit(solution)/shard_map/reduce_scatter | solution.py:639
  343.6 1.0 convert_element_type.80
  344.6 0.8 copy.129
  (194 shorter events, 23.5 us)
Async XLA Ops:
  7.2 16.9 %copy-start.9 = (bf16[2,12,2304]{2,0,1:T(2,128)(2,1)S(1)}, bf16[2,12,2304]{2,0,1:T(2,128)(2,1)}, u32[]{:S(2)}) copy-start(bf16[2,12,2304]{2,0,1:T(2,128)(2,1)} %param.16) | copy-start | bytes 331780
  7.2 128.2 %all-gather.3.cloned.1.call-start = ((), (), s32[]{:S(2)}) async-start(), calls=%async_computation.14 | async-start | bytes 3649536 | tf_op jit(solution)/shard_map/all_gather | solution.py:598
  12.5 1.4 copy-start.23
  12.5 1.4 copy-start.25
  13.9 9.5 %all-to-all-start.1 = ((bf16[4,2,384]{2,1,0:T(2,128)(2,1)}), bf16[4,2,384]{2,1,0:T(2,128)(2,1)S(1)}, u32[]{:S(2)}, u32[]{:S(2)}) async-start(bf16[4,2,384]{2,1,0:T(2,128)(2,1)} %broadcast_in_dim.120), calls=%async_computation.1 | async-start | bytes 12288 | tf_op jit(solution)/shard_map/all_to_all | solution.py:516
  19.5 0.9 copy-start.30
  23.4 0.6 copy-start.27
  24.6 20.0 %copy-start.32 = (s32[2]{0:T(128)S(1)}, s32[2]{0:T(128)}, u32[]{:S(2)}) copy-start(s32[2]{0:T(128)} %live.1) | copy-start | bytes 28
  24.6 20.0 %copy-start.1 = (bf16[2,2,256,384]{3,2,1,0:T(8,128)(2,1)S(1)}, bf16[2,2,256,384]{3,2,1,0:T(8,128)(2,1)}, u32[]{:S(2)}) copy-start(bf16[2,2,256,384]{3,2,1,0:T(8,128)(2,1)} %refs_1_.1) | copy-start | bytes 2359300
  25.7 12.6 %all-to-all-start.2 = ((f32[32,1,1488]{2,1,0:T(1,128)}), f32[32,1,1488]{2,1,0:T(1,128)S(1)}, u32[]{:S(2)}, u32[]{:S(2)}) async-start(f32[32,1,1488]{2,1,0:T(1,128)} %copy.105), calls=%async_computation.2 | async-start | bytes 393216 | tf_op jit(solution)/shard_map/all_to_all | solution.py:516
  39.0 17.2 %all-to-all-start = ((bf16[4,16,3456]{2,1,0:T(8,128)(2,1)}), bf16[4,16,3456]{2,1,0:T(8,128)(2,1)S(1)}, u32[]{:S(2)}, u32[]{:S(2)}) async-start(bf16[4,16,3456]{2,1,0:T(8,128)(2,1)} %broadcast_in_dim.119), calls=%async_computation | async-start | bytes 884736 | tf_op jit(solution)/shard_map/all_to_all | solution.py:516
  45.8 0.6 copy-start.15
  56.9 30.7 %all-to-all-start.3 = ((f32[8,1,1152]{2,1,0:T(1,128)}), f32[8,1,1152]{2,1,0:T(1,128)S(1)}, u32[]{:S(2)}, u32[]{:S(2)}) async-start(f32[8,1,1152]{2,1,0:T(1,128)} %broadcast_in_dim.124), calls=%async_computation.3 | async-start | bytes 73728 | tf_op jit(solution)/shard_map/all_to_all | solution.py:516
  60.2 14.2 %collective-permute-start = (bf16[4,16,3456]{2,1,0:T(8,128)(2,1)S(1)}, bf16[4,16,3456]{2,1,0:T(8,128)(2,1)S(1)}, u32[]{:S(2)}, u32[]{:S(2)}) collective-permute-start(bf16[4,16,3456]{2,1,0:T(8,128)(2,1)S(1)} %all-to-all-done), channel_id=1, source_target_pairs={{0,2},{1,5},{2,0},{3,7},{4,6},{5,1},{6,4},{7,3},{8,10},{9,13},{10,... | collective-permute-start | bytes 1327112 | tf_op jit(solution)/shard_map/ppermute | solution.py:500
  74.5 21.0 %copy-start.5 = (bf16[8,16,3456]{2,1,0:T(8,128)(2,1)}, bf16[8,16,3456]{2,1,0:T(8,128)(2,1)S(1)}, u32[]{:S(2)}) copy-start(bf16[8,16,3456]{2,1,0:T(8,128)(2,1)S(1)} %constant_dynamic-update-slice_fusion.refs_0_) | copy-start | bytes 2654212
  74.5 13.1 %collective-permute-start.1 = (bf16[8,16,3456]{2,1,0:T(8,128)(2,1)S(1)}, bf16[8,16,3456]{2,1,0:T(8,128)(2,1)S(1)}, u32[]{:S(2)}, u32[]{:S(2)}) collective-permute-start(bf16[8,16,3456]{2,1,0:T(8,128)(2,1)S(1)} %constant_dynamic-update-slice_fusion.refs_0_), channel_id=1, source_target_pairs={{0,4},{1,3},{2,6},{3,1},{4,0},{5,7},{6,2},{7,5},{8,12},{9,11},{10,... | collective-permute-start | bytes 2654216 | tf_op jit(solution)/shard_map/ppermute | solution.py:500
  76.0 19.4 %collective-permute-start.2 = (bf16[8,16,3456]{2,1,0:T(8,128)(2,1)S(1)}, bf16[8,16,3456]{2,1,0:T(8,128)(2,1)S(1)}, u32[]{:S(2)}, u32[]{:S(2)}) collective-permute-start(bf16[8,16,3456]{2,1,0:T(8,128)(2,1)S(1)} %constant_dynamic-update-slice_fusion.refs_0_), channel_id=1, source_target_pairs={{0,1},{1,0},{2,3},{3,2},{4,5},{5,4},{6,7},{7,6},{8,9},{9,8},{10,11... | collective-permute-start | bytes 2654216 | tf_op jit(solution)/shard_map/ppermute | solution.py:500
  87.6 7.9 %copy-start.6 = (bf16[8,16,3456]{2,1,0:T(8,128)(2,1)}, bf16[8,16,3456]{2,1,0:T(8,128)(2,1)S(1)}, u32[]{:S(2)}) copy-start(bf16[8,16,3456]{2,1,0:T(8,128)(2,1)S(1)} %collective-permute-done.1.refs_1_) | copy-start | bytes 2654212
  87.6 7.9 %collective-permute-start.3 = (bf16[8,16,3456]{2,1,0:T(8,128)(2,1)S(1)}, bf16[8,16,3456]{2,1,0:T(8,128)(2,1)}, u32[]{:S(2)}, u32[]{:S(2)}) collective-permute-start(bf16[8,16,3456]{2,1,0:T(8,128)(2,1)S(1)} %collective-permute-done.1.refs_1_), channel_id=1, source_target_pairs={{0,1},{1,0},{2,3},{3,2},{4,5},{5,4},{6,7},{7,6},{8,9},{9,8},{10,11... | collective-permute-start | bytes 2654216 | tf_op jit(solution)/shard_map/ppermute | solution.py:500
  87.6 31.0 %all-to-all-start.5 = ((bf16[8,2,2,32,384]{4,3,2,1,0:T(8,128)(2,1)}), bf16[8,2,2,32,384]{4,3,2,1,0:T(8,128)(2,1)S(1)}, u32[]{:S(2)}, u32[]{:S(2)}) async-start(bf16[8,2,2,32,384]{4,3,2,1,0:T(8,128)(2,1)} %bitcast.103), calls=%async_computation.5 | async-start | bytes 1572864 | tf_op jit(solution)/shard_map/all_to_all | solution.py:516
  95.4 1.0 copy-start.7
  96.4 26.4 %copy-start.20 = (s32[32,16]{1,0:T(8,128)S(1)}, s32[32,16]{1,0:T(8,128)}, u32[]{:S(2)}) copy-start(s32[32,16]{1,0:T(8,128)} %get-tuple-element.139) | copy-start | bytes 6148
  96.4 26.5 %copy-start.19 = (s32[32,16]{1,0:T(8,128)S(1)}, s32[32,16]{1,0:T(8,128)}, u32[]{:S(2)}) copy-start(s32[32,16]{1,0:T(8,128)} %get-tuple-element.138) | copy-start | bytes 6148
  96.4 26.5 %copy-start.18 = (s32[32,16]{1,0:T(8,128)S(1)}, s32[32,16]{1,0:T(8,128)}, u32[]{:S(2)}) copy-start(s32[32,16]{1,0:T(8,128)} %get-tuple-element.142) | copy-start | bytes 6148
  96.4 26.6 %copy-start.17 = (s32[32,16]{1,0:T(8,128)S(1)}, s32[32,16]{1,0:T(8,128)}, u32[]{:S(2)}) copy-start(s32[32,16]{1,0:T(8,128)} %get-tuple-element.135) | copy-start | bytes 6148
  96.4 26.7 %copy-start.16 = (s32[4,512]{1,0:T(4,128)S(1)}, s32[4,512]{1,0:T(4,128)}, u32[]{:S(2)}) copy-start(s32[4,512]{1,0:T(4,128)} %copy-done.15) | copy-start | bytes 24580
  118.6 17.3 %copy-start.3 = (bf16[8,2,2,32,384]{4,3,2,1,0:T(8,128)(2,1)}, bf16[8,2,2,32,384]{4,3,2,1,0:T(8,128)(2,1)S(1)}, u32[]{:S(2)}) copy-start(bf16[8,2,2,32,384]{4,3,2,1,0:T(8,128)(2,1)S(1)} %all-to-all-done.5.refs_2_) | copy-start | bytes 2359300
  118.6 16.7 %all-to-all-start.4 = ((bf16[8,2,2,32,384]{4,3,2,1,0:T(8,128)(2,1)}), bf16[8,2,2,32,384]{4,3,2,1,0:T(8,128)(2,1)S(1)}, u32[]{:S(2)}, u32[]{:S(2)}) async-start(bf16[8,2,2,32,384]{4,3,2,1,0:T(8,128)(2,1)} %get-tuple-element.35), calls=%async_computation.4 | async-start | bytes 1572864 | tf_op jit(solution)/shard_map/all_to_all | solution.py:516
  123.1 12.8 %copy-start.13 = (s32[8,512]{1,0:T(8,128)}, s32[8,512]{1,0:T(8,128)S(1)}, u32[]{:S(2)}) copy-start(s32[8,512]{1,0:T(8,128)S(1)} %stack.88.row_map) | copy-start | bytes 49156
  135.4 0.9 copy-start.4
  136.3 59.8 %copy-start.12 = (s32[8,512]{1,0:T(8,128)S(1)}, s32[8,512]{1,0:T(8,128)}, u32[]{:S(2)}) copy-start(s32[8,512]{1,0:T(8,128)} %stack.87.row_map) | copy-start | bytes 49156
  192.4 16.1 %all-to-all-start.7 = ((bf16[8,2,2,32,384]{4,3,2,1,0:T(8,128)(2,1)}), bf16[8,2,2,32,384]{4,3,2,1,0:T(8,128)(2,1)S(1)}, u32[]{:S(2)}, u32[]{:S(2)}) async-start(bf16[8,2,2,32,384]{4,3,2,1,0:T(8,128)(2,1)} %get-tuple-element.37), calls=%async_computation.7 | async-start | bytes 1572864 | tf_op jit(solution)/shard_map/all_to_all | solution.py:516
  196.0 147.6 %reduce-scatter.2.cloned.1.call-start = ((), (), s32[]{:S(2)}) async-start(), calls=%async_computation.13 | async-start | bytes 3649536 | tf_op jit(solution)/shard_map/reduce_scatter | solution.py:639
  208.5 0.9 copy-start.2
  239.8 6.2 %collective-permute-start.4 = (bf16[16,16,3456]{2,1,0:T(8,128)(2,1)S(1)}, bf16[16,16,3456]{2,1,0:T(8,128)(2,1)}, u32[]{:S(2)}, u32[]{:S(2)}) collective-permute-start(bf16[16,16,3456]{2,1,0:T(8,128)(2,1)S(1)} %slice.245), channel_id=1, source_target_pairs={{0,1},{1,0},{2,3},{3,2},{4,5},{5,4},{6,7},{7,6},{8,9},{9,8},{10,11... | collective-permute-start | bytes 5308424 | tf_op jit(solution)/shard_map/ppermute | solution.py:500
  239.9 0.7 copy-start.21
  239.9 0.7 copy-start.22
  242.0 13.8 %all-to-all-start.8 = ((f32[8,2,576]{2,1,0:T(2,128)}), f32[8,2,576]{2,1,0:T(2,128)}, u32[]{:S(2)}, u32[]{:S(2)}) async-start(f32[8,2,576]{2,1,0:T(2,128)} %copy.117), calls=%async_computation.8 | async-start | bytes 81920 | tf_op jit(solution)/shard_map/all_to_all | solution.py:516
  248.5 2.1 copy-start.14
  248.5 2.1 copy-start.28
  248.5 2.0 copy-start.29
  248.6 14.0 %collective-permute-start.5 = (bf16[8,16,3456]{2,1,0:T(8,128)(2,1)S(1)}, bf16[8,16,3456]{2,1,0:T(8,128)(2,1)S(1)}, u32[]{:S(2)}, u32[]{:S(2)}) collective-permute-start(bf16[8,16,3456]{2,1,0:T(8,128)(2,1)S(1)} %slice.286), channel_id=1, source_target_pairs={{0,4},{1,3},{2,6},{3,1},{4,0},{5,7},{6,2},{7,5},{8,12},{9,11},{10,... | collective-permute-start | bytes 2654216 | tf_op jit(solution)/shard_map/ppermute | solution.py:500
  255.8 16.9 %all-to-all-start.6 = ((bf16[8,2,2,32,384]{4,3,2,1,0:T(8,128)(2,1)}), bf16[8,2,2,32,384]{4,3,2,1,0:T(8,128)(2,1)}, u32[]{:S(2)}, u32[]{:S(2)}) async-start(bf16[8,2,2,32,384]{4,3,2,1,0:T(8,128)(2,1)} %get-tuple-element.36), calls=%async_computation.6 | async-start | bytes 1572864 | tf_op jit(solution)/shard_map/all_to_all | solution.py:516
  262.6 14.2 %copy-start.33 = (s32[2]{0:T(128)S(1)}, s32[2]{0:T(128)}, u32[]{:S(2)}) copy-start(s32[2]{0:T(128)} %live.1) | copy-start | bytes 28
  263.6 30.1 %collective-permute-start.6 = (bf16[4,16,3456]{2,1,0:T(8,128)(2,1)}, bf16[4,16,3456]{2,1,0:T(8,128)(2,1)}, u32[]{:S(2)}, u32[]{:S(2)}) collective-permute-start(bf16[4,16,3456]{2,1,0:T(8,128)(2,1)} %slice.288), channel_id=1, source_target_pairs={{0,2},{1,5},{2,0},{3,7},{4,6},{5,1},{6,4},{7,3},{8,10},{9,13},{10,... | collective-permute-start | bytes 1327112 | tf_op jit(solution)/shard_map/ppermute | solution.py:500
  272.8 12.1 %all-to-all-start.9 = ((f32[32,1,1488]{2,1,0:T(1,128)}), f32[32,1,1488]{2,1,0:T(1,128)S(1)}, u32[]{:S(2)}, u32[]{:S(2)}) async-start(f32[32,1,1488]{2,1,0:T(1,128)} %all_to_all.58), calls=%async_computation.9 | async-start | bytes 393216 | tf_op jit(solution)/shard_map/all_to_all | solution.py:516
  278.1 10.1 %copy-start.10 = (bf16[2,12,2304]{2,0,1:T(2,128)(2,1)S(1)}, bf16[2,12,2304]{2,0,1:T(2,128)(2,1)}, u32[]{:S(2)}) copy-start(bf16[2,12,2304]{2,0,1:T(2,128)(2,1)} %param.16) | copy-start | bytes 331780
  284.9 0.7 copy-start.8
  285.6 19.1 %copy-start = (bf16[2,2,256,384]{3,2,1,0:T(8,128)(2,1)S(1)}, bf16[2,2,256,384]{3,2,1,0:T(8,128)(2,1)}, u32[]{:S(2)}) copy-start(bf16[2,2,256,384]{3,2,1,0:T(8,128)(2,1)} %refs_0_.1) | copy-start | bytes 2359300
  290.3 9.6 %all-to-all-start.10 = ((f32[32,2,12]{2,1,0:T(2,128)}), f32[32,2,12]{2,1,0:T(2,128)S(1)}, u32[]{:S(2)}, u32[]{:S(2)}) async-start(f32[32,2,12]{2,1,0:T(2,128)} %bitcast.42), calls=%async_computation.10 | async-start | bytes 65536 | tf_op jit(solution)/shard_map/all_to_all | solution.py:516
  299.9 17.2 %all-to-all-start.11 = ((bf16[4,16,3456]{2,1,0:T(8,128)(2,1)}), bf16[4,16,3456]{2,1,0:T(8,128)(2,1)S(1)}, u32[]{:S(2)}, u32[]{:S(2)}) async-start(bf16[4,16,3456]{2,1,0:T(8,128)(2,1)} %add_convert_fusion.2), calls=%async_computation.11 | async-start | bytes 884736 | tf_op jit(solution)/shard_map/all_to_all | solution.py:516
  304.7 6.6 %copy-start.24 = (f32[2,192]{1,0:T(2,128)S(1)}, f32[2,192]{1,0:T(2,128)}, u32[]{:S(2)}) copy-start(f32[2,192]{1,0:T(2,128)} %copy-done.23) | copy-start | bytes 4612
  304.7 6.6 %copy-start.26 = (f32[2,192]{1,0:T(2,128)S(1)}, f32[2,192]{1,0:T(2,128)}, u32[]{:S(2)}) copy-start(f32[2,192]{1,0:T(2,128)} %copy-done.25) | copy-start | bytes 4612
  304.7 6.7 %copy-start.31 = (bf16[2,384]{1,0:T(2,128)(2,1)S(1)}, bf16[2,384]{1,0:T(2,128)(2,1)}, u32[]{:S(2)}) copy-start(bf16[2,384]{1,0:T(2,128)(2,1)} %param.12) | copy-start | bytes 4612
  343.6 4.7 %copy-start.11 = (bf16[16,3456]{1,0:T(8,128)(2,1)S(1)}, bf16[16,3456]{1,0:T(8,128)(2,1)}, u32[]{:S(2)}) copy-start(bf16[16,3456]{1,0:T(8,128)(2,1)} %reduce-scatter.2.cloned.1.call-done) | copy-start | bytes 331780
Sparse Core Ops, SparseCore 0:
  11.9 68.7 all-gather.2
  240.0 103.5 reduce-scatter.1
